TPU v7x, 128 devices: a whole 4x4x4 slice. The times are simulated.
128 devices in a mesh: fsdp: 4 (over z), ctx: 4 (over x), tp: 8 (over y, core).
Axes of the slice: x: 4, y: 4, z: 4, core: 2. Of those that a mesh axis runs over, the one named last changes fastest.
Arguments:
- inputs: bfloat16 [4, 1024, 2048], P('fsdp', 'ctx'), may hold values from -6 to 6
- cotangent: bfloat16 [4, 1024, 2048], P('fsdp', 'ctx'), may hold values from -6 to 6
- segment_ids: int32 [4, 1024], P('fsdp'), may hold values from 0 to 2, as said below
- w_query: bfloat16 [2, 2048, 1024], P(None, ('fsdp', 'ctx'), 'tp'), may hold values from -0.125 to 0.125
- w_shared: bfloat16 [2, 2048, 1024], P(None, ('fsdp', 'ctx')), may hold values from -0.125 to 0.125
- w_zx: bfloat16 [2, 2048, 2, 3072], P(None, ('fsdp', 'ctx'), None, 'tp'), may hold values from -0.125 to 0.125
- w_dt: bfloat16 [2, 2048, 48], P(None, ('fsdp', 'ctx'), 'tp'), may hold values from -0.125 to 0.125
- w_attn_out: bfloat16 [2, 2048, 1024], P(None, ('fsdp', 'ctx'), 'tp'), may hold values from -0.75 to 0.75
- w_ssm_out: bfloat16 [2, 2048, 3072], P(None, ('fsdp', 'ctx'), 'tp'), may hold values from -0.109375 to 0.109375
- w_gate: bfloat16 [2, 2048, 4096], P(None, ('fsdp', 'ctx'), 'tp'), may hold values from -0.125 to 0.125
- w_up: bfloat16 [2, 2048, 4096], P(None, ('fsdp', 'ctx'), 'tp'), may hold values from -0.125 to 0.125
- w_down: bfloat16 [2, 2048, 4096], P(None, ('fsdp', 'ctx'), 'tp'), may hold values from -0.09375 to 0.09375
- gains: float32 [2, 2, 2048], replicated, may hold values from 0.5 to 1.5
- conv_x: float32 [2, 5, 3072], P(None, None, 'tp'), may hold values from -3 to 3
- conv_bc: float32 [2, 5, 512], replicated, may hold values from -3 to 3
- head_params: float32 [2, 3, 48], P(None, None, 'tp'), may hold values from -7 to 2
Outputs:
- layer_out: bfloat16 [4, 1024, 2048], P('fsdp', 'ctx')
- input_grad: float32 [4, 1024, 2048], P('fsdp', 'ctx')
- grad_w_query: float32 [2, 2048, 1024], P(None, ('fsdp', 'ctx'), 'tp')
- grad_w_shared: float32 [2, 2048, 1024], P(None, ('fsdp', 'ctx'))
- grad_w_zx: float32 [2, 2048, 2, 3072], P(None, ('fsdp', 'ctx'), None, 'tp')
- grad_w_dt: float32 [2, 2048, 48], P(None, ('fsdp', 'ctx'), 'tp')
- grad_w_attn_out: float32 [2, 2048, 1024], P(None, ('fsdp', 'ctx'), 'tp')
- grad_w_ssm_out: float32 [2, 2048, 3072], P(None, ('fsdp', 'ctx'), 'tp')
- grad_w_gate: float32 [2, 2048, 4096], P(None, ('fsdp', 'ctx'), 'tp')
- grad_w_up: float32 [2, 2048, 4096], P(None, ('fsdp', 'ctx'), 'tp')
- grad_w_down: float32 [2, 2048, 4096], P(None, ('fsdp', 'ctx'), 'tp')
- grad_gains: float32 [2, 2048], replicated
- grad_conv_x: float32 [2, 5, 3072], P(None, None, 'tp')
- grad_conv_bc: float32 [2, 5, 512], replicated
- grad_head_params: float32 [2, 2, 48], P(None, None, 'tp')
- grad_ffn_gains: float32 [2, 2048], replicated
- grad_skip: float32 [2, 48], P(None, 'tp')
Inputs may be any that keep to these rules, and one draw needn't show every extreme that they name: `segment_ids`: each row never falls; document 1 begins within the first 256 places and ends within the last 256 places.
All inputs are finite; a program needn't handle non-finite values.
Results may differ from a plain program's by a relative error of at most 0.035.
Values may be sent and summed in bfloat16 or wider, within the bound.
No kernel may reach another device: no remote copies, remote signals or barrier semaphores. Data moves between devices by JAX's collectives and lax.ppermute only.
A program may use at most 256 MiB of HBM per device.

v0:
```python
import math
from functools import partial

import jax
import jax.numpy as jnp
from jax import lax
from jax.experimental import pallas as pl
from jax.experimental.pallas import tpu as pltpu
from jax.sharding import PartitionSpec as P

HD = 128
HP = 64
NSTATE = 256
CONV = 4
ROWS = 256
SHARE = 32
XLOC = 384
PROJ = 1152
LATE = 640
HLOC = 6
PAIRS = 3
SEQ_BLOCKS = 4
MSG = XLOC + 16
KV = 128
VMEM_LIMIT = 16 * 1024 * 1024

norm_eps = 1e-05
rope_base = 100000000000.0
bf16 = jnp.bfloat16
f32 = jnp.float32
i32 = jnp.int32


def along_y(value, steps):
    pairs = [(i, ((i // 2 + steps) % 4) * 2 + i % 2) for i in range(8)]
    return lax.ppermute(value, "tp", pairs)


def other_core(value):
    return lax.ppermute(value, "tp", [(i, i ^ 1) for i in range(8)])


def along_ctx(value, steps):
    first, last = max(0, -steps), min(4, 4 - steps)
    return lax.ppermute(value, "ctx", [(i, i + steps) for i in range(first, last)])


def ring(value, axis, steps):
    return lax.ppermute(value, axis, [(i, (i + steps) % 4) for i in range(4)])


def from_all(value, beside=None):
    half = [value] + [along_y(value, -k) for k in (1, 2, 3)]
    if beside is not None:
        half[1], beside = lax.optimization_barrier((half[1], beside))
    parts = tuple(half + [other_core(part) for part in half])
    return parts if beside is None else (parts, beside)


def dot_nn(a, b):
    return jnp.dot(a, b, preferred_element_type=f32)


def dot_nt(a, b):
    return lax.dot_general(a, b, (((1,), (1,)), ((), ())), preferred_element_type=f32)


def dot_tn(a, b):
    return lax.dot_general(a, b, (((0,), (0,)), ((), ())), preferred_element_type=f32)


def shape_of(shape, dtype=f32):
    return jax.ShapeDtypeStruct(shape, dtype)


class Columns:
    def __init__(self, array, block=0, width=None, rows=None, keep=False):
        self.array, self.block, self.keep = array, block, keep
        self.shape = (rows or array.shape[0],) + array.shape[1:-1] + (width or array.shape[-1],)

    def spec(self):
        place = (0,) * (len(self.shape) - 1) + (self.block,)
        return pl.BlockSpec(self.shape, lambda i: place, pipeline_mode=pl.Buffered(1))


class Layer:
    def __init__(self, array, layer):
        self.array, self.layer, self.keep = array, layer, True
        self.shape = (1,) + array.shape[1:]

    def spec(self):
        place = (self.layer,) + (0,) * (len(self.shape) - 1)
        return pl.BlockSpec(self.shape, lambda i: place, pipeline_mode=pl.Buffered(1))


def stored(array):
    return Columns(array, keep=True)


def summands(parts):
    return [stored(parts[0])] + passed(parts[1:])


def passed(arrays):
    return [Columns(array) for array in arrays]


def kept(shape, dtype=f32):
    return pltpu.HBM(shape, dtype)


def fetch_kernel(places, *refs):
    count = len(places)
    sources, outs, sems = refs[:count], refs[count : 2 * count], refs[-1]
    copies = []
    for (start, pieces), source, out in zip(places, sources, outs):
        rows, width = out.shape[0] // pieces, out.shape[1]
        for index in range(pieces):
            own = pl.ds(rows * index, rows)
            copies.append(
                pltpu.make_async_copy(
                    source.at[own, pl.ds(start, width)], out.at[own, :], sems.at[len(copies)]
                )
            )
    for copy in copies:
        copy.start()
    for copy in copies:
        copy.wait()


def fetched_all(name, sources):
    places = [(start, 4 if array.shape[0] == 2048 and width > 128 else 1) for array, start, width in sources]
    whole = pl.BlockSpec(memory_space=pltpu.VMEM)
    return pl.pallas_call(
        partial(fetch_kernel, places),
        name=name,
        out_shape=tuple(pltpu.VMEM((array.shape[0], width), array.dtype) for array, _, width in sources),
        in_specs=[pl.BlockSpec(memory_space=pltpu.HBM)] * len(sources),
        out_specs=tuple(whole for _ in sources),
        scratch_shapes=[pltpu.SemaphoreType.DMA((sum(pieces for _, pieces in places),))],
        compiler_params=pltpu.CompilerParams(vmem_limit_bytes=VMEM_LIMIT),
        cost_estimate=pl.CostEstimate(
            flops=0, bytes_accessed=sum(2 * array.shape[0] * width for array, _, width in sources), transcendentals=0
        ),
    )(*(pltpu.with_memory_space_constraint(array, pltpu.HBM) for array, _, _ in sources))


def fetched(name, array, start, width):
    return fetched_all(name, [(array, start, width)])[0]


def restored(name, arrays):
    return fetched_all(name, [(array, 0, array.shape[1]) for array in arrays])


def run_kernel(kernel, outs, flags, *args, scratch=(), us=1.0):
    whole = pl.BlockSpec(memory_space=pltpu.VMEM)
    own = [isinstance(arg, (Columns, Layer)) for arg in args]
    specs, arrays, out_specs = [], [], []
    for arg, copied in zip(args, own):
        specs.append(arg.spec() if copied else whole)
        array = arg.array if copied else arg
        arrays.append(pltpu.with_memory_space_constraint(array, pltpu.HBM) if copied and arg.keep else array)
    for out in outs:
        in_vmem = isinstance(out, jax.ShapeDtypeStruct)
        out_specs.append(whole if in_vmem else pl.BlockSpec(out.shape, lambda i, n=len(out.shape): (0,) * n))
        own.append(not in_vmem)
    moved = sum(2 * math.prod(arg.shape) for arg in args) + sum(2 * math.prod(o.shape) for o in outs)
    if flags is not None:
        specs = [pl.BlockSpec(memory_space=pltpu.SMEM)] + specs
        arrays = [flags] + arrays
    return pl.pallas_call(
        kernel,
        grid=(1,) if any(own) else (),
        out_shape=tuple(outs),
        in_specs=specs,
        out_specs=tuple(out_specs),
        scratch_shapes=list(scratch),
        compiler_params=pltpu.CompilerParams(vmem_limit_bytes=VMEM_LIMIT),
        cost_estimate=pl.CostEstimate(flops=int(us * 1e9), bytes_accessed=moved, transcendentals=0),
    )(*arrays)


def local_block(flags, natural):
    return pl.multiple_of(flags[8 + natural] * SHARE, SHARE)


def rank_block(flags, rank):
    return pl.multiple_of(flags[16 + rank] * ROWS, ROWS)


def lane_index(shape):
    return lax.broadcasted_iota(i32, shape, len(shape) - 1)


def spread(columns, pair):
    low = lane_index((1, 128)) < HP
    return jnp.where(low, columns[:, 2 * pair : 2 * pair + 1], columns[:, 2 * pair + 1 : 2 * pair + 2])


def lanes_of(pair):
    return slice(128 * pair, 128 * pair + 128)


def turned(value, table, sign):
    return value * table[:, 0:128] + sign * (pltpu.roll(value, 64, 1) * table[:, 128:256])


def segments(table):
    return table[:, 259:260]


def sigmoid(v):
    return 1.0 / (1.0 + jnp.exp(-v))


def softplus(v):
    return jnp.maximum(v, 0.0) + jnp.log1p(jnp.exp(-jnp.abs(v)))


def conv_sum(ext, table, weight):
    total = weight[CONV : CONV + 1, :] + ext[8 : 8 + ROWS, :] * weight[3:4, :]
    for tap in range(CONV - 1):
        total = total + table[:, 256 + tap : 257 + tap] * ext[5 + tap : 5 + tap + ROWS, :] * weight[tap : tap + 1, :]
    return total


def conv_back(grad_out, ext, table, weight, work, grad_ref, edge_ref, gweight_ref):
    total = conv_sum(ext, table, weight)
    sig = sigmoid(total)
    grad = grad_out * sig * (1.0 + total * (1.0 - sig))
    width = grad.shape[1]
    gweight_ref[...] = jnp.zeros((8, width), f32)
    gweight_ref[CONV : CONV + 1, :] = jnp.sum(grad, axis=0, keepdims=True)
    gweight_ref[3:4, :] = jnp.sum(grad * ext[8 : 8 + ROWS, :], axis=0, keepdims=True)
    work[0:8, :] = jnp.zeros((8, width), f32)
    work[264:272, :] = jnp.zeros((8, width), f32)
    own = grad * weight[3:4, :]
    edge = jnp.zeros((8, width), f32)
    for tap in range(CONV - 1):
        part = grad * table[:, 256 + tap : 257 + tap]
        gweight_ref[tap : tap + 1, :] = jnp.sum(
            part * ext[5 + tap : 5 + tap + ROWS, :], axis=0, keepdims=True
        )
        work[8:264, :] = part * weight[tap : tap + 1, :]
        own = own + work[11 - tap : 11 - tap + ROWS, :]
        edge = edge + work[3 - tap : 11 - tap, :]
    grad_ref[...] = own
    edge_ref[...] = edge


def pack_kernel(place, *refs):
    out, at, index = refs[-1], 0, 0
    while index < len(refs) - 1:
        ref = refs[index]
        if len(ref.shape) == 4:
            out[:, at : at + XLOC] = ref[0, :, 0, :]
            out[:, at + XLOC : at + 512] = refs[index + 1][0]
            out[:, at + 512 : at + 896] = ref[0, :, 1, :]
            at, index = at + 896, index + 2
            continue
        width = min(ref.shape[2], 512)
        if width == HLOC:
            out[:, at : at + 128] = jnp.zeros((out.shape[0], 128), bf16)
            out[:, at : at + HLOC] = ref[0]
            width = 128
        elif ref.shape[2] == 1024:
            width = 128
            out[:, at : at + width] = ref[0, :, pl.ds(pl.multiple_of(place[0] * 128, 128), 128)]
        else:
            out[:, at : at + width] = ref[0]
        at, index = at + width, index + 1


def first_kernel(flags, rows, cotangent, gain, normed, inverse, hidden_kept, grads, grad):
    for block in range(8):
        own = slice(SHARE * block, SHARE * (block + 1))
        from_rows = pl.ds(pl.multiple_of(flags[24 + block] * SHARE, SHARE), SHARE)
        wide = rows[0, from_rows, :].astype(f32)
        scale = lax.rsqrt(jnp.mean(wide * wide, axis=1, keepdims=True) + norm_eps)
        normed[own, :] = (wide * scale * gain[0:1, :]).astype(bf16)
        grads[own, :] = cotangent[0, from_rows, :]
        if block == 0:
            hidden_kept[...] = wide
            inverse[...] = jnp.broadcast_to(scale, inverse.shape)
            grad[...] = cotangent[0, from_rows, :].astype(f32)


def joined(parts):
    return parts[0][...] if len(parts) == 1 else jnp.concatenate([part[...] for part in parts], axis=0)


def projections(flags, work, table, z, z_kept, xs, query, query_kept, dtn, dtn_kept):
    for block in range(8):
        own = slice(SHARE * block, SHARE * (block + 1))
        from_rows = pl.ds(local_block(flags, block), SHARE)
        for out in (z, z_kept):
            out[own, :] = work[from_rows, 0:XLOC]
        xs[own, 0:XLOC] = work[from_rows, 512:896]
        xs[own, XLOC:512] = work[from_rows, 1024:PROJ]
        head = turned(work[from_rows, XLOC:512], table[own, :], 1.0).astype(bf16)
        for out in (query, query_kept):
            out[own, :] = head
        for out in (dtn, dtn_kept):
            out[own, :] = work[from_rows, 896:1024]


def proj_kernel(flags, p0, p1, p2, p3, p4, p5, p6, p7, weight, table, normed, *refs):
    rows = joined((p0, p1, p2, p3, p4, p5, p6, p7))
    normed[...] = rows
    work = refs[-1]
    work[...] = dot_nn(rows, weight[...])
    projections(flags, work, table, *refs[:-1])


def first_proj_kernel(flags, rows, weight, table, z, z_kept, xs, query, query_kept, dtn, dtn_kept, work):
    step = pl.program_id(0)
    part = dot_nn(rows[...], weight[...])

    @pl.when(step == 0)
    def _():
        work[...] = part

    @pl.when(step > 0)
    def _():
        work[...] = work[...] + part

    @pl.when(step == 3)
    def _():
        projections(flags, work, table, z, z_kept, xs, query, query_kept, dtn, dtn_kept)


def first_projections(flags, normed, weight, table):
    model = normed.shape[1]
    whole = pl.BlockSpec(memory_space=pltpu.VMEM)
    outs = [
        shape_of((ROWS, XLOC)), kept((ROWS, XLOC)), shape_of((ROWS, 512)), shape_of((ROWS, HD), bf16),
        kept((ROWS, HD), bf16), shape_of((ROWS, 128)), kept((ROWS, 128)),
    ]
    return pl.pallas_call(
        first_proj_kernel,
        grid=(4,),
        out_shape=tuple(outs),
        in_specs=[
            pl.BlockSpec(memory_space=pltpu.SMEM),
            pl.BlockSpec((ROWS, model // 4), lambda i: (0, i)),
            pl.BlockSpec((model // 4, PROJ), lambda i: (i, 0)),
            whole,
        ],
        out_specs=tuple(
            whole if isinstance(out, jax.ShapeDtypeStruct) else pl.BlockSpec(out.shape, lambda i: (0, 0))
            for out in outs
        ),
        scratch_shapes=[pltpu.VMEM((ROWS, PROJ), f32)],
        compiler_params=pltpu.CompilerParams(vmem_limit_bytes=VMEM_LIMIT),
        cost_estimate=pl.CostEstimate(flops=4 * 10**9, bytes_accessed=2 * model * PROJ, transcendentals=0),
    )(flags, normed, pltpu.with_memory_space_constraint(weight, pltpu.HBM), table)


def shared_kernel(flags, xs, halo, table, small, out, ext):
    own = xs[:, XLOC:512]
    ext[0:8, :] = halo[:, XLOC:512]
    ext[8 : 8 + ROWS, :] = own
    total = conv_sum(ext, table, small[:, XLOC:512])
    rank = flags[0]
    out[...] = jnp.where(
        rank < 2, turned(own, table, 1.0), jnp.where(rank < 4, own, total * sigmoid(total))
    ).astype(bf16)


def prep_kernel(xs, dtn, halo, table, small, ext, xc, xc_kept, rates, rates_kept, rates_t, rates_t_kept):
    ext[0:8, :] = halo[:, 0:XLOC]
    ext[8 : 8 + ROWS, :] = xs[:, 0:XLOC]
    total = conv_sum(ext, table, small[:, 0:XLOC])
    for out in (xc, xc_kept):
        out[...] = total * sigmoid(total)
    params = small[:, 512:640]
    rate = softplus(dtn[...] + params[1:2, :])
    logs = -jnp.exp(params[0:1, :]) * rate
    rows = lax.broadcasted_iota(i32, (ROWS, ROWS), 0)
    lower = (rows >= lane_index((ROWS, ROWS))).astype(f32)
    running = jnp.dot(lower, logs, precision=lax.Precision.HIGHEST, preferred_element_type=f32)
    for out in (rates, rates_kept):
        out[:, 0:128] = rate
        out[:, 128:256] = running
    rate_t, running_t = rate.T[0:8, :], running.T[0:8, :]
    for out in (rates_t, rates_t_kept):
        out[0:8, :] = rate_t
        out[8:16, :] = running_t


def block_decays(flags, rates_t):
    kept = jnp.where(flags[4] == flags[5], 1.0, 0.0)
    return jnp.exp(rates_t[8:16, ROWS - 1 : ROWS]) * kept


def decay_rows(flags, rates_t):
    rows = jnp.broadcast_to(block_decays(flags, rates_t), (8, NSTATE))
    return jnp.concatenate([rows, jnp.zeros((8, NSTATE), f32)], axis=0).astype(bf16)


def weights_in(rates, table):
    last = rates[ROWS - 1 : ROWS, 128:256]
    gap = jnp.exp(last - rates[:, 128:256]) * table[:, 261:262]
    return gap, gap * rates[:, 0:128]


def rank_columns(flags, shared, first):
    return jnp.concatenate(
        [shared[pl.ds(rank_block(flags, rank), ROWS), :] for rank in (first, first + 1)], axis=1
    )


def inject_of(flags, shared):
    return rank_columns(flags, shared, 4)


def readout_of(flags, shared):
    return rank_columns(flags, shared, 6)


def carry_of(rates, table):
    return jnp.exp(rates[:, 128:256]) * table[:, 260:261]


def state_kernel(flags, s0, s1, s2, s3, s4, s5, s6, s7, xc, rates, rates_t, table, out, shared, shared_kept):
    for index, part in enumerate((s0, s1, s2, s3, s4, s5, s6, s7)):
        shared[ROWS * index : ROWS * (index + 1), :] = part[...]
        shared_kept[ROWS * index : ROWS * (index + 1), :] = part[...]
    inject = inject_of(flags, shared)
    _, weight = weights_in(rates, table)
    for pair in range(PAIRS):
        weighted = (xc[:, lanes_of(pair)] * spread(weight, pair)).astype(bf16)
        out[KV + 128 * pair : KV + 128 * (pair + 1), :] = dot_tn(weighted, inject).astype(bf16)
    out[KV + XLOC : KV + MSG, :] = decay_rows(flags, rates_t)
    half = shared[pl.ds(rank_block(flags, 2 * flags[2] + flags[1] // 2), ROWS), :]
    out[0:KV, :] = jnp.concatenate([half[0:128], half[128:256]], axis=1)


def halves_kernel(msg1, msg2, msg3, out):
    for index, msg in enumerate((msg1, msg2, msg3)):
        out[KV * index : KV * (index + 1), :] = msg[...]


def allowed_pairs(table, seg_rows):
    rows = lax.broadcasted_iota(i32, (ROWS, ROWS), 0)
    return (rows >= lane_index((ROWS, ROWS))) & (segments(table) == seg_rows[0:1, :])


def head_decay(allowed, rates, rates_t, head):
    gap = rates[:, 128 + head : 129 + head] - rates_t[8 + head : 9 + head, :]
    return jnp.where(allowed, jnp.exp(jnp.where(allowed, gap, 0.0)), 0.0)


def intra_kernel(flags, shared, xc, rates, rates_t, table, seg_rows, small, out):
    inject, readout = inject_of(flags, shared), readout_of(flags, shared)
    both = dot_nt(readout, inject)
    allowed = allowed_pairs(table, seg_rows)
    low = lane_index((1, 128)) < HP
    for pair in range(PAIRS):
        x = xc[:, lanes_of(pair)]
        xb = x.astype(bf16)
        heads = []
        for head in (2 * pair, 2 * pair + 1):
            decay = head_decay(allowed, rates, rates_t, head)
            heads.append(dot_nn((both * decay * rates_t[head : head + 1, :]).astype(bf16), xb))
        out[:, lanes_of(pair)] = jnp.where(low, heads[0], heads[1]) + spread(small[2:3, 512:640], pair) * x


def keys_values(flags, shared, halves, swapped):
    head, first = flags[1] // 2, flags[2] == 0
    pairs = [
        (
            shared[pl.ds(rank_block(flags, head), ROWS), :],
            shared[pl.ds(rank_block(flags, 2 + head), ROWS), :],
        )
    ]
    for index, half in enumerate(halves):
        packed = half[...], swapped[KV * index : KV * (index + 1), :]
        mine, theirs = (jnp.concatenate([part[:, 0:128], part[:, 128:256]], axis=0) for part in packed)
        pairs.append((jnp.where(first, mine, theirs), jnp.where(first, theirs, mine)))
    return pairs


def masked_scores(query, pairs, table, seg_rows):
    parts = []
    for block, (keys, _) in enumerate(pairs):
        score = dot_nt(query, keys) * HD ** (-0.5)
        keep = segments(table) == seg_rows[block : block + 1, :]
        if block == 0:
            rows = lax.broadcasted_iota(i32, (ROWS, ROWS), 0)
            keep = keep & (rows >= lane_index((ROWS, ROWS)))
        parts.append(jnp.where(keep, score, -1e30))
    return parts


def attention_kernel(flags, query, shared, h1, h2, h3, swapped, table, seg_rows, out, out_kept, log_total, kept):
    pairs = keys_values(flags, shared, (h1, h2, h3), swapped)
    for block, (keys, values) in enumerate(pairs):
        kept[ROWS * block : ROWS * (block + 1), 0:HD] = keys
        kept[ROWS * block : ROWS * (block + 1), HD : 2 * HD] = values
    parts = masked_scores(query[...], pairs, table, seg_rows)
    top = parts[0].max(axis=1, keepdims=True)
    for part in parts[1:]:
        top = jnp.maximum(top, part.max(axis=1, keepdims=True))
    parts = [jnp.exp(part - top) for part in parts]
    total = sum(part.sum(axis=1, keepdims=True) for part in parts)
    inverse = 1.0 / total
    result = jnp.zeros((ROWS, HD), f32)
    for part, (_, values) in zip(parts, pairs):
        result = result + dot_nn((part * inverse).astype(bf16), values)
    rounded = result.astype(bf16)
    for block in range(8):
        for ref in (out, out_kept):
            ref[pl.ds(local_block(flags, block), SHARE), :] = rounded[SHARE * block : SHARE * (block + 1), :]
    log_total[...] = jnp.broadcast_to(top + jnp.log(total), (ROWS, HD))


def chained(first, second, third, base):
    rows1 = first[base + XLOC : base + MSG, :].astype(f32)
    rows2 = second[base + XLOC : base + MSG, :].astype(f32)
    parts = []
    for head in range(HLOC):
        own = slice(base + HP * head, base + HP * head + HP)
        older = second[own, :].astype(f32) + rows2[head : head + 1, :] * third[own, :].astype(f32)
        parts.append(first[own, :].astype(f32) + rows1[head : head + 1, :] * older)
    return jnp.concatenate(parts, axis=0)


def carry_kernel(flags, msg1, msg2, msg3, shared, rates, table, intra, z, state, ssm_y, cat, cat_kept):
    entering = chained(msg1, msg2, msg3, KV)
    state[...] = entering
    from_state = dot_nt(readout_of(flags, shared), entering.astype(bf16))
    carry = carry_of(rates, table)
    for pair in range(PAIRS):
        own = lanes_of(pair)
        y = intra[:, own] + spread(carry, pair) * from_state[:, own]
        ssm_y[:, own] = y
        gate = z[:, own]
        gated = (y * gate * sigmoid(gate)).astype(bf16)
        for block in range(8):
            for out in (cat, cat_kept):
                out[pl.ds(local_block(flags, block), SHARE), 128 * pair : 128 * (pair + 1)] = gated[
                    SHARE * block : SHARE * (block + 1), :
                ]


def gate_back_kernel(
    flags, p0, p1, p2, p3, p4, p5, p6, p7, weight, z, ssm_y, shared, rates, rates_t, table,
    dmix, dattn, dy, dz, msg, work, local,
):
    rows = joined((p0, p1, p2, p3, p4, p5, p6, p7))
    dmix[...] = rows
    local[...] = dot_nn(rows, weight[...])
    for block in range(8):
        own = slice(SHARE * block, SHARE * (block + 1))
        from_rows = pl.ds(local_block(flags, block), SHARE)
        dattn[own, :] = local[from_rows, 0:128].astype(bf16)
        work[own, :] = local[from_rows, 128:512]
    readout = readout_of(flags, shared)
    carry = carry_of(rates, table)
    for pair in range(PAIRS):
        own = lanes_of(pair)
        gate, grad = z[:, own], work[:, own]
        sig = sigmoid(gate)
        y_grad = grad * gate * sig
        dy[:, own] = y_grad
        dz[:, own] = (grad * ssm_y[:, own] * sig * (1.0 + gate * (1.0 - sig))).astype(bf16)
        msg[own, :] = dot_tn((y_grad * spread(carry, pair)).astype(bf16), readout).astype(bf16)
    msg[XLOC:MSG, :] = decay_rows(flags, rates_t)


def attention_back_kernel(
    flags, dattn, dz, query, kept, log_total, table, seg_rows,
    early, mine, theirs,
):
    pairs = []
    for block in range(SEQ_BLOCKS):
        own = slice(ROWS * block, ROWS * (block + 1))
        pairs.append((kept[own, 0:HD], kept[own, HD : 2 * HD]))
    first = flags[2] == 0
    q = query[...]
    grad = dattn[...]
    parts = masked_scores(q, pairs, table, seg_rows)
    logs = log_total[:, 0:1]
    probs = [jnp.exp(part - logs) for part in parts]
    grads = [dot_nt(grad, values) for _, values in pairs]
    inner = sum((p * g).sum(axis=1, keepdims=True) for p, g in zip(probs, grads))
    total = jnp.zeros((ROWS, HD), f32)
    for block, (p, g, (keys, _)) in enumerate(zip(probs, grads, pairs)):
        own = slice(ROWS * block, ROWS * (block + 1))
        score = (p * (g - inner)).astype(bf16)
        total = total + dot_nn(score, keys)
        dkeys = dot_tn(score, q) * HD ** (-0.5)
        dvalues = dot_tn(p.astype(bf16), grad)
        mine[own, :] = jnp.where(first, dkeys, dvalues)
        theirs[own, :] = jnp.where(first, dvalues, dkeys).astype(bf16)
    total = total * HD ** (-0.5)
    dq = turned(total, table, -1.0).astype(bf16)
    for block in range(8):
        own = slice(SHARE * block, SHARE * (block + 1))
        to_rows = pl.ds(local_block(flags, block), SHARE)
        early[to_rows, 0:XLOC] = dz[own, :]
        early[to_rows, XLOC:512] = dq[own, :]


def intra_back_kernel(
    flags, dy, xc, shared, rates, rates_t, table, seg_rows, state, small,
    dx, dshared, drates, dskip, row_sums, dcum,
):
    inject, readout = inject_of(flags, shared), readout_of(flags, shared)
    both = dot_nt(readout, inject)
    allowed = allowed_pairs(table, seg_rows)
    low = lane_index((1, 128)) < HP
    carry = carry_of(rates, table)
    entering = state[...].astype(bf16)
    from_state = dot_nt(readout, entering)
    dboth = jnp.zeros((ROWS, ROWS), f32)
    row_sums[...] = jnp.zeros((128, ROWS), f32)
    dcum[...] = jnp.zeros((ROWS, 128), f32)
    carried = []
    for pair in range(PAIRS):
        own = lanes_of(pair)
        x = xc[:, own]
        xb = x.astype(bf16)
        grad = dy[:, own]
        dskip[:, own] = jnp.sum(grad * x, axis=0, keepdims=True)
        carried.append((grad * spread(carry, pair)).astype(bf16))
        through = grad * from_state[:, own]
        total = spread(small[2:3, 512:640], pair) * grad
        for head in (2 * pair, 2 * pair + 1):
            mine = low if head % 2 == 0 else jnp.logical_not(low)
            decay = head_decay(allowed, rates, rates_t, head)
            steps = rates_t[head : head + 1, :]
            head_grad = jnp.where(mine, grad, 0.0).astype(bf16)
            dmix = dot_nt(head_grad, xb)
            kept = dmix * decay
            dboth = dboth + kept * steps
            mixed = both * decay
            total = total + dot_tn((mixed * steps).astype(bf16), head_grad)
            passed = dmix * mixed
            row_sums[head : head + 1, :] = jnp.sum(passed, axis=0, keepdims=True)
            dcum[:, head : head + 1] = jnp.sum(passed * steps, axis=1, keepdims=True) + carry[
                :, head : head + 1
            ] * jnp.sum(jnp.where(mine, through, 0.0), axis=1, keepdims=True)
        dx[:, own] = total
    columns = row_sums[...].T
    drates[:, 0:128] = columns
    drates[:, 128:256] = dcum[...] - rates[:, 0:128] * columns
    dboth_b = dboth.astype(bf16)
    dshared[:, NSTATE:] = dot_nn(dboth_b, inject) + dot_nn(jnp.concatenate(carried, axis=1), entering)
    dshared[:, 0:NSTATE] = dot_tn(dboth_b, readout)


def packed_back_kernel(
    flags, msg1, msg2, msg3, shared, xc, rates, table, dshared, kv0, kv1, kv2, kv3, packed, state_grad,
):
    later = chained(msg1, msg2, msg3, 0)
    state_grad[...] = later
    _, weights = weights_in(rates, table)
    weighted = [(xc[:, lanes_of(pair)] * spread(weights, pair)).astype(bf16) for pair in range(PAIRS)]
    weighted = jnp.concatenate(weighted, axis=1)
    dinject = (dshared[:, 0:NSTATE] + dot_nn(weighted, later.astype(bf16))).astype(bf16)
    dreadout = dshared[:, NSTATE:].astype(bf16)
    packed[...] = jnp.zeros((8 * ROWS, 128), bf16)
    grads = kv0[...] + kv1[...].astype(f32) + kv2[...].astype(f32) + kv3[...].astype(f32)
    owner = 2 * flags[2] + flags[1] // 2
    packed[pl.ds(rank_block(flags, owner), ROWS), :] = grads.astype(bf16)
    packed[pl.ds(rank_block(flags, 4), ROWS), :] = dinject[:, 0:128]
    packed[pl.ds(rank_block(flags, 5), ROWS), :] = dinject[:, 128:256]
    packed[pl.ds(rank_block(flags, 6), ROWS), :] = dreadout[:, 0:128]
    packed[pl.ds(rank_block(flags, 7), ROWS), :] = dreadout[:, 128:256]


def state_back_kernel(
    flags, later, shared, xc, rates, rates_t, table, state, small, dtn, dx, drates, ext,
    dxpre, edge, gweight, ddt, heads, work, dconv, sums,
):
    inject = inject_of(flags, shared)
    low = lane_index((1, 128)) < HP
    params = small[:, 512:640]
    gap, weights = weights_in(rates, table)
    from_later = dot_nt(inject, later[...].astype(bf16))
    products = later[...] * state[...]
    decays = block_decays(flags, rates_t)
    sums[...] = jnp.zeros((ROWS, 128), f32)
    for pair in range(PAIRS):
        own = lanes_of(pair)
        dconv[:, own] = dx[:, own] + spread(weights, pair) * from_later[:, own]
        through = xc[:, own] * from_later[:, own]
        for head in (2 * pair, 2 * pair + 1):
            mine = low if head % 2 == 0 else jnp.logical_not(low)
            sums[:, head : head + 1] = jnp.sum(jnp.where(mine, through, 0.0), axis=1, keepdims=True)
    dweights = sums[...]
    moved = dweights * weights
    last = jnp.sum(moved, axis=0, keepdims=True)
    lanes = lane_index((1, 128))
    for head in range(HLOC):
        total = jnp.sum(
            jnp.sum(products[HP * head : HP * head + HP, :], axis=0, keepdims=True), axis=1, keepdims=True
        )
        last = last + jnp.where(lanes == head, total * decays[head : head + 1, :], 0.0)
    rows = lax.broadcasted_iota(i32, (ROWS, 128), 0)
    dcums = drates[:, 128:256] - moved + jnp.where(rows == ROWS - 1, last, 0.0)
    square = lax.broadcasted_iota(i32, (ROWS, ROWS), 0)
    upper = (square <= lane_index((ROWS, ROWS))).astype(f32)
    dlogs = jnp.dot(upper, dcums, precision=lax.Precision.HIGHEST, preferred_element_type=f32)
    rate = -jnp.exp(params[0:1, :])
    dsteps = drates[:, 0:128] + dweights * gap + dlogs * rate
    ddts = dsteps * sigmoid(dtn[...] + params[1:2, :])
    ddt[...] = ddts
    heads[...] = jnp.zeros((8, 128), f32)
    heads[0:1, :] = jnp.sum(dlogs * rate * rates[:, 0:128], axis=0, keepdims=True)
    heads[1:2, :] = jnp.sum(ddts, axis=0, keepdims=True)
    conv_back(dconv[...], ext, table, small[:, 0:XLOC], work, dxpre, edge, gweight)


def shared_back_kernel(flags, part0, part1, part2, part3, ext, table, small, out, edge, gweight, work):
    grad = part0[...] + part1[...].astype(f32) + part2[...].astype(f32) + part3[...].astype(f32)
    conv_back(grad, ext, table, small[:, XLOC:512], work, out, edge, gweight)
    rank = flags[0]
    of_conv = jnp.where(rank < 4, 0.0, 1.0)
    edge[...] = edge[...] * of_conv
    gweight[...] = gweight[...] * of_conv
    out[...] = jnp.where(rank < 2, turned(grad, table, -1.0), jnp.where(rank < 4, grad, out[...]))


def late_kernel(flags, dxpre, edge_x, dsh, edge_sh, ddt, out):
    for block in range(8):
        own = slice(SHARE * block, SHARE * (block + 1))
        to_rows = pl.ds(local_block(flags, block), SHARE)
        x, sh = dxpre[own, :], dsh[own, :]
        if block == 7:
            pad = jnp.zeros((SHARE - 8, 128), f32)
            sh = sh + jnp.concatenate([pad, edge_sh[...]], axis=0)
            x = x + jnp.concatenate([jnp.zeros((SHARE - 8, XLOC), f32), edge_x[...]], axis=0)
        out[to_rows, 0:XLOC] = x.astype(bf16)
        out[to_rows, 512:LATE] = sh.astype(bf16)
        out[to_rows, XLOC:512] = jnp.where(lane_index((1, 128)) < HLOC, ddt[own, :], 0.0).astype(bf16)


def half_sum_kernel(own, other, keep, send1, send2, send3):
    rows = own.shape[0] // 4
    keep[...] = own[0:rows, :] + other[0:rows, :].astype(f32)
    for index, send in ((1, send1), (2, send2), (3, send3)):
        part = slice(rows * index, rows * (index + 1))
        send[...] = (own[part, :].astype(f32) + other[part, :].astype(f32)).astype(bf16)


def parts_of_sum(own, other, along, sign):
    return parts_from(own, other_core(other), along, sign)


def parts_from(own, got, along, sign):
    rows, width = own.shape[0] // 4, own.shape[1]
    sent = shape_of((rows, width), bf16)
    keep, *sends = run_kernel(half_sum_kernel, [kept((rows, width)), sent, sent, sent], None, own, Columns(got))
    return (keep,) + tuple(along(send, sign * k) for k, send in zip((1, 2, 3), sends))


def split_kernel(*refs):
    lefts, weight, own, other = refs[:-3], refs[-3], refs[-2], refs[-1]
    left = lefts[0][...] if len(lefts) == 1 else jnp.concatenate([ref[...] for ref in lefts], axis=1)
    result = dot_nt(left, weight[...])
    own[...] = result[: ROWS // 2]
    other[...] = result[ROWS // 2 :].astype(bf16)


def summed_rows(lefts, weight):
    model, width = weight.shape
    own, other = pl.pallas_call(
        split_kernel,
        grid=(model // 512,),
        out_shape=(shape_of((ROWS // 2, model)), shape_of((ROWS // 2, model), bf16)),
        in_specs=[pl.BlockSpec(left.shape, lambda i: (0, 0)) for left in lefts]
        + [pl.BlockSpec((512, width), lambda i: (i, 0))],
        out_specs=(
            pl.BlockSpec((ROWS // 2, 512), lambda i: (0, i)),
            pl.BlockSpec((ROWS // 2, 512), lambda i: (0, i)),
        ),
        compiler_params=pltpu.CompilerParams(vmem_limit_bytes=VMEM_LIMIT),
        cost_estimate=pl.CostEstimate(
            flops=2 * ROWS * model * width, bytes_accessed=2 * model * width, transcendentals=0
        ),
    )(*lefts, weight)
    return parts_of_sum(own, other, along_y, 1)


def gate_up_kernel(p0, p1, p2, p3, p4, p5, p6, p7, weight, normed, gate, up, act, act_kept):
    rows = joined((p0, p1, p2, p3, p4, p5, p6, p7))
    normed[...] = rows
    result = dot_nn(rows, weight[...])
    g, u = result[:, :512], result[:, 512:]
    gate[...] = g
    up[...] = u
    for out in (act, act_kept):
        out[...] = (g * sigmoid(g) * u).astype(bf16)


def gate_up_back_kernel(*refs):
    parts, (weight, gate, up, dffn, out) = refs[:-5], refs[-5:]
    rows = joined(parts)
    dffn[...] = rows
    dact = dot_nn(rows, weight[...])
    g = gate[...]
    sig = sigmoid(g)
    out[:, :512] = (dact * up[...] * sig * (1.0 + g * (1.0 - sig))).astype(bf16)
    out[:, 512:] = (dact * g * sig).astype(bf16)


def natural_kernel(flags, p0, p1, p2, p3, p4, p5, p6, p7, out):
    local = joined((p0, p1, p2, p3, p4, p5, p6, p7)).astype(out.dtype)
    for block in range(8):
        out[pl.ds(pl.multiple_of(flags[24 + block] * SHARE, SHARE), SHARE), :] = local[
            SHARE * block : SHARE * (block + 1), :
        ]


def add_norm_kernel(hidden, part0, part1, part2, part3, gain, out_kept, normed, inverse):
    total = hidden[...] + part0[...] + (
        part1[...].astype(f32) + part2[...].astype(f32) + part3[...].astype(f32)
    )
    out_kept[...] = total
    scale = lax.rsqrt(jnp.mean(total * total, axis=1, keepdims=True) + norm_eps)
    inverse[...] = jnp.broadcast_to(scale, inverse.shape)
    normed[...] = (total * scale * gain[...]).astype(bf16)


def add_norm(hidden, parts, gain):
    shape = hidden.shape
    return run_kernel(
        add_norm_kernel,
        [kept(shape), shape_of(shape, bf16), kept((shape[0], 128))],
        None, hidden, *summands(parts), gain[None],
    )


def output_kernel(hidden, part0, part1, part2, part3, out):
    total = hidden[...] + part0[...] + (
        part1[...].astype(f32) + part2[...].astype(f32) + part3[...].astype(f32)
    )
    out[...] = total.astype(bf16)


def norm_back_kernel(grad, part0, part1, part2, part3, hidden, inverse, gain, out, rounded, ggain):
    received = part0[...] + (part1[...].astype(f32) + part2[...].astype(f32) + part3[...].astype(f32))
    scale = inverse[:, 0:1]
    unit = hidden[...] * scale
    scaled = received * gain[...]
    ggain[...] = jnp.sum(received * unit, axis=0, keepdims=True)
    total = grad[...] + scale * (scaled - unit * jnp.mean(scaled * unit, axis=1, keepdims=True))
    out[...] = total
    rounded[...] = total.astype(bf16)


def norm_back(parts, grad, hidden, inverse, gain):
    shape = hidden.shape
    return run_kernel(
        norm_back_kernel,
        [kept(shape), shape_of(shape, bf16), kept((1, shape[1]))],
        None, grad, *summands(parts), hidden, inverse, gain[None],
    )


def gradient_kernel(pairs, *refs):
    out, at = refs[-1], 0
    for index in range(pairs):
        left, right = refs[2 * index], refs[2 * index + 1]
        width = right.shape[1]
        out[:, at : at + width] = dot_tn(left[...], right[...]).astype(bf16)
        at += width
    if at < out.shape[1]:
        out[:, at:] = jnp.zeros((out.shape[0], out.shape[1] - at), bf16)


def weight_gradients(pairs, total, block, index, buffer=None):
    rows, model = pairs[0][0].shape
    width = sum(right.shape[1] for _, right in pairs)
    specs, args = [], []
    for left, right in pairs:
        block_right = right.block if isinstance(right, Columns) else 0
        specs += [
            pl.BlockSpec((rows, 512), lambda i: (0, i)),
            pl.BlockSpec(right.shape, lambda i, block=block_right: (0, block)),
        ]
        args += [left, right.array if isinstance(right, Columns) else right]
    aliases = {}
    kernel = partial(gradient_kernel, len(pairs))
    if buffer is not None:
        aliases = {len(args): 0}
        specs.append(pl.BlockSpec(memory_space=pltpu.HBM))
        args.append(buffer)

        def kernel(*refs):
            gradient_kernel(len(pairs), *refs[:-2], refs[-1])

    return pl.pallas_call(
        kernel,
        grid=(model // 512,),
        out_shape=pltpu.HBM((model, total), bf16),
        in_specs=specs,
        out_specs=pl.BlockSpec((512, block), lambda i: (i, index)),
        input_output_aliases=aliases,
        compiler_params=pltpu.CompilerParams(vmem_limit_bytes=VMEM_LIMIT),
        cost_estimate=pl.CostEstimate(
            flops=2 * rows * model * width, bytes_accessed=model * width * 2, transcendentals=0
        ),
    )(*args)


def owned_kernel(pairs, *refs):
    out, at = refs[-1], 0
    for pair in range(pairs):
        left, right = refs[2 * pair], refs[2 * pair + 1]
        result = dot_tn(left[...], right[...]).astype(bf16)
        width = right.shape[1]
        for index in range(2):
            out[index, :, at : at + width] = result[128 * index : 128 * (index + 1)]
        at += width


def insert_kernel(small, block, out):
    mine = lane_index((1, 1, 128)) < HLOC
    out[...] = jnp.where(mine, block[...], small[...][None])


def with_small(owned, small):
    spec = pl.BlockSpec((16, 128, 128), lambda i: (0, 0, XLOC // 128))
    return pl.pallas_call(
        insert_kernel,
        grid=(1,),
        out_shape=pltpu.HBM(owned.shape, bf16),
        in_specs=[pl.BlockSpec((128, 128), lambda i: (0, 0)), spec],
        out_specs=spec,
        input_output_aliases={1: 0},
        compiler_params=pltpu.CompilerParams(vmem_limit_bytes=VMEM_LIMIT),
        cost_estimate=pl.CostEstimate(flops=10**9, bytes_accessed=10**6, transcendentals=0),
    )(small, owned)


def owned_gradients(pairs):
    rows, model = pairs[0][0].shape
    width = sum(right.shape[1] for _, right in pairs)
    specs, args = [], []
    for left, right in pairs:
        block = right.block if isinstance(right, Columns) else 0
        specs += [
            pl.BlockSpec((rows, 256), lambda i: (0, i)),
            pl.BlockSpec(right.shape, lambda i, block=block: (0, block)),
        ]
        args += [left, right.array if isinstance(right, Columns) else right]
    return pl.pallas_call(
        partial(owned_kernel, len(pairs)),
        grid=(model // 256,),
        out_shape=pltpu.HBM((16, model // 16, width), bf16),
        in_specs=specs,
        out_specs=pl.BlockSpec((2, model // 16, width), lambda i: (i, 0, 0)),
        compiler_params=pltpu.CompilerParams(vmem_limit_bytes=VMEM_LIMIT),
        cost_estimate=pl.CostEstimate(
            flops=2 * rows * model * width, bytes_accessed=model * width * 2, transcendentals=0
        ),
    )(*args)


def small_kernel(gain1, gain2, conv_sh, conv_x, heads, skip, out):
    out[...] = jnp.zeros(out.shape, bf16)
    for row in range(16):
        own = slice(128 * row, 128 * row + 128)
        out[row : row + 1, :] = gain1[:, own].astype(bf16)
        out[16 + row : 17 + row, :] = gain2[:, own].astype(bf16)
    out[32:37, :] = conv_sh[0:5, :].astype(bf16)
    for tap in range(CONV + 1):
        for pair in range(PAIRS):
            row = 37 + PAIRS * tap + pair
            out[row : row + 1, :] = conv_x[tap : tap + 1, lanes_of(pair)].astype(bf16)
    out[52:54, :] = heads[0:2, :].astype(bf16)
    lanes = lane_index((1, 128))
    sums = jnp.zeros((1, 128), f32)
    for pair in range(PAIRS):
        part = skip[:, lanes_of(pair)]
        for half in range(2):
            mine = (lanes < HP) if half == 0 else (lanes >= HP)
            total = jnp.sum(jnp.where(mine, part, 0.0), axis=1, keepdims=True)
            sums = sums + jnp.where(lanes == 2 * pair + half, total, 0.0)
    out[54:55, :] = sums.astype(bf16)


def spread_kernel(small, out, work):
    work[...] = small[...].astype(f32)
    columns = work[...].T
    work[56:62, :] = columns[122:128, :]
    out[...] = pltpu.roll(work[...], HLOC, 1).astype(bf16)


def gathered_back(packed, work):
    rolled = pltpu.roll(packed, 128 - HLOC, 1)
    work[...] = jnp.zeros((128, 128), f32)
    work[122:128, :] = rolled[56:62, :]
    return jnp.where(lane_index((1, 128)) < 128 - HLOC, rolled, work[...].T)


def owner_sum(values):
    total = values[0].astype(f32)
    for index in range(1, 16):
        total = total + values[index].astype(f32)
    return total


def block_sum_kernel(values, over_tp, late, conv_x, heads, work):
    whole = owner_sum(values)
    late[...] = whole[:, 0:LATE]
    total = gathered_back(whole[:, XLOC:512], work)
    over_tp[0:128, :] = whole[:, 512:LATE].astype(bf16)
    over_tp[128:256, :] = whole[:, LATE : LATE + 128].astype(bf16)
    over_tp[256:352, :] = jnp.zeros((96, 128), bf16)
    for layer in range(2):
        first = 64 * layer
        over_tp[256 + 48 * layer : 293 + 48 * layer, :] = total[first : first + 37, :].astype(bf16)
        for tap in range(CONV + 1):
            for pair in range(PAIRS):
                row = first + 37 + PAIRS * tap + pair
                conv_x[5 * layer + tap : 5 * layer + tap + 1, lanes_of(pair)] = total[row : row + 1, :]
        heads[3 * layer : 3 * layer + 3, :] = total[first + 52 : first + 55, :]


def weight_outputs_kernel(lower, upper, late, attn, ssm, gate, up, down, query, zx, dt):
    for layer, ref in ((0, lower), (1, upper)):
        for index, out in enumerate((gate, up, down)):
            out[layer] = ref[:, 512 * index : 512 * (index + 1)].astype(f32)
        attn[layer] = ref[:, 1536:1664].astype(f32)
        ssm[layer] = ref[:, 1664:2048].astype(f32)
        zx[layer, :, 0, :] = ref[:, 2048:2432].astype(f32)
        query[layer] = ref[:, 2432:2560].astype(f32)
    zx[0, :, 1, :] = late[:, 0:XLOC]
    zx[1, :, 1, :] = lower[:, 2560:2944].astype(f32)
    dt[0] = late[:, XLOC : XLOC + HLOC]
    dt[1] = lower[:, 2944 : 2944 + HLOC].astype(f32)


def tp_outputs_kernel(flags, *refs):
    parts, (shared, gains1, gains2, conv_bc, every) = refs[:8], refs[8:]
    total = jnp.zeros((96, 128), f32)
    for index, part in enumerate(parts):
        every[index] = part[...].astype(f32)
        total = total + part[256:352, :].astype(f32)
    for layer in range(2):
        for rank in range(8):
            own = slice(128 * rank, 128 * rank + 128)
            shared[layer, :, own] = every[flags[16 + rank], 128 * layer : 128 * layer + 128, :]
        for row in range(16):
            own = slice(128 * row, 128 * row + 128)
            at = 48 * layer + row
            gains1[layer : layer + 1, own] = total[at : at + 1, :]
            gains2[layer : layer + 1, own] = total[at + 16 : at + 17, :]
        for rank in range(4):
            part = every[flags[20 + rank], 288 + 48 * layer : 296 + 48 * layer, :]
            conv_bc[5 * layer : 5 * layer + 5, 128 * rank : 128 * rank + 128] = part[0:5, :]


def body(
    inputs, cotangent, segment_ids, w_query, w_shared, w_zx, w_dt, w_attn_out, w_ssm_out, w_gate, w_up, w_down,
    gains, conv_x, conv_bc, head_params,
):
    layers = w_query.shape[0]
    rank, ctx = lax.axis_index("tp"), lax.axis_index("ctx")
    y, core = rank // 2, rank % 2
    model = inputs.shape[2]

    def local_of(block_y, block_core):
        return jnp.where(block_core == core, 0, 4) + (block_y - y) % 4

    seg_all = segment_ids[0]
    first_row = ctx * ROWS
    padded = jnp.concatenate([jnp.full((CONV - 1,), -1, i32), seg_all])
    seg_ext = lax.dynamic_slice_in_dim(padded, first_row, ROWS + CONV - 1)
    seg_own = seg_ext[CONV - 1 :]
    blocks = seg_all.reshape(SEQ_BLOCKS, ROWS)
    seg_rows = jnp.stack(
        [
            jnp.where(ctx >= back, lax.dynamic_index_in_dim(blocks, jnp.maximum(ctx - back, 0), 0, False), -1)
            for back in range(SEQ_BLOCKS)
        ]
        + [jnp.full((ROWS,), -1, i32)] * 4
    ).astype(f32)
    naturals = jnp.arange(8, dtype=i32)
    flags = jnp.concatenate(
        [
            jnp.stack([rank, y, core, ctx, seg_ext[CONV - 2], seg_own[-1], rank, rank]).astype(i32),
            local_of(naturals % 4, naturals // 4).astype(i32),
            local_of(naturals // 2, naturals % 2).astype(i32),
            (jnp.where(naturals < 4, core, 1 - core) * 4 + (y + naturals) % 4).astype(i32),
        ]
    )

    half_width = HD // 2
    frequency = rope_base ** (-jnp.arange(half_width, dtype=f32) / half_width)
    places = (first_row + jnp.arange(ROWS, dtype=i32)).astype(f32)
    angles = places[:, None] * frequency[None, :]
    cosine, sine = jnp.cos(angles), jnp.sin(angles)
    marks = [seg_ext[tap : tap + ROWS] == seg_own for tap in range(CONV - 1)]
    marks += [seg_own, seg_own == seg_ext[CONV - 2], seg_own == seg_own[-1]]
    marks = jnp.pad(jnp.stack([mark.astype(f32) for mark in marks], axis=1), ((0, 0), (0, 122)))
    table = jnp.concatenate([cosine, cosine, -sine, sine, marks], axis=1)

    own_conv = jnp.maximum(rank - 4, 0) * 128
    small = []
    for layer in range(layers):
        rows = [conv_x[layer], lax.dynamic_slice_in_dim(conv_bc[layer], own_conv, 128, 1)]
        rows.append(jnp.pad(head_params[layer], ((0, 2), (0, 128 - HLOC))))
        small.append(jnp.pad(jnp.concatenate(rows, axis=1), ((0, 3), (0, 0))))

    def packed(*members):
        width = sum(
            {4: 2 * XLOC}.get(member.ndim, 128 if member.shape[2] in (1024, HLOC) else member.shape[2])
            for member, _ in members
        )
        (columns,) = run_kernel(
            pack_kernel,
            [shape_of((w_query.shape[1], width), bf16)],
            rank.astype(i32).reshape(1),
            *(Layer(member, layer) for member, layer in members),
        )
        return lax.all_gather(columns, ("fsdp", "ctx"), axis=0, tiled=True)

    def proj_members(layer):
        return [(member, layer) for member in (w_zx, w_query, w_dt, w_shared)]

    weight_a = packed(*proj_members(0), (w_attn_out, 0), (w_ssm_out, 0))
    weight_b = packed(*proj_members(1), (w_gate, 0), (w_up, 0), (w_down, 0))
    weight_c = packed((w_gate, 1), (w_up, 1), (w_down, 1), (w_attn_out, 1), (w_ssm_out, 1))
    proj_place = [(weight_a, 0, PROJ), (weight_b, 0, PROJ)]
    out_place = [(weight_a, PROJ, 512), (weight_c, 1536, 512)]
    gate_up_place = [(weight_b, PROJ, 1024), (weight_c, 0, 1024)]
    down_place = [(weight_b, PROJ + 1024, 512), (weight_c, 1024, 512)]

    def together(*values):
        return lax.optimization_barrier(values)

    weight_a, table, seg_rows, small = together(weight_a, table, seg_rows, small)
    normed_shape = shape_of((ROWS, model), bf16)
    normed_kept = kept((ROWS, model), bf16)
    normed_b, inverse1, hidden, dffn_b, grad_hidden = run_kernel(
        first_kernel,
        [normed_kept, kept((SHARE, 128)), kept((SHARE, model)), normed_kept, kept((SHARE, model))],
        flags, inputs, cotangent, gains[0],
    )
    weight_a, normed_b = together(weight_a, normed_b)
    proj_place[0] = (weight_a, 0, PROJ)
    out_place[0] = (weight_a, PROJ, 512)
    dffn_parts = (dffn_b,)
    saved = []
    wide = shape_of((ROWS, 512))
    for layer in range(layers):
        if layer == 0:
            z, z_kept, xs, query, query_kept, dtn, dtn_kept = first_projections(flags, normed_b, weight_a, table)
        else:
            normed_b, z, z_kept, xs, query, query_kept, dtn, dtn_kept = run_kernel(
                proj_kernel,
                [
                    normed_kept, shape_of((ROWS, XLOC)), kept((ROWS, XLOC)), wide, shape_of((ROWS, HD), bf16),
                    kept((ROWS, HD), bf16), shape_of((ROWS, 128)), kept((ROWS, 128)),
                ],
                flags, *passed(normed_parts), proj_weight, table,
                scratch=[pltpu.VMEM((ROWS, PROJ), f32)], us=3.3,
            )
        halo = along_ctx(xs[ROWS - 8 :], 1)
        shared_own, shared_ext = run_kernel(
            shared_kernel,
            [shape_of((ROWS, 128), bf16), kept((264, 128))],
            flags, xs, Columns(halo), table, small[layer],
        )
        prepared = run_kernel(
            prep_kernel,
            [
                kept((264, XLOC)), shape_of((ROWS, XLOC)), kept((ROWS, XLOC)), shape_of((ROWS, 256)),
                kept((ROWS, 256)), shape_of((16, ROWS)), kept((16, ROWS)),
            ],
            None, xs, dtn, Columns(halo), table, small[layer], us=1.5,
        )
        shared_parts, prepared = from_all(shared_own, prepared)
        x_ext, xc, xc_kept, rates, rates_kept, rates_t, rates_t_kept = prepared
        message, shared, shared_kept = run_kernel(
            state_kernel,
            [shape_of((KV + MSG, NSTATE), bf16), shape_of((8 * ROWS, 128), bf16), kept((8 * ROWS, 128), bf16)],
            flags, *passed(shared_parts), xc, rates, rates_t, table, us=1.9,
        )
        earlier = tuple(along_ctx(message, back) for back in (1, 2, 3))
        (intra,) = run_kernel(
            intra_kernel, [shape_of((ROWS, XLOC))],
            flags, shared, xc, rates, rates_t, table, seg_rows, small[layer], us=1.3,
        )
        if layer > 0:
            earlier, intra = together(earlier, intra)
        else:
            earlier, intra, out_weight = together(earlier, intra, fetched(f"out_{layer}", *out_place[layer]))
        halves = [Columns(part, 0, NSTATE, rows=KV) for part in earlier]
        (swapped,) = run_kernel(halves_kernel, [shape_of((3 * KV, NSTATE), bf16)], None, *halves)
        state, ssm_y, gated, gated_kept = run_kernel(
            carry_kernel,
            [kept((XLOC, NSTATE)), kept((ROWS, XLOC)), shape_of((ROWS, XLOC), bf16), kept((ROWS, XLOC), bf16)],
            flags, *passed(earlier), shared, rates, table, intra, z, us=1.9,
        )
        swapped, gated = together(other_core(swapped), gated)
        attn, attn_kept, log_total, pairs = run_kernel(
            attention_kernel,
            [
                shape_of((ROWS, HD), bf16), kept((ROWS, HD), bf16), kept((ROWS, HD)),
                kept((SEQ_BLOCKS * ROWS, 2 * HD), bf16),
            ],
            flags, query, shared, *halves, Columns(swapped), table, seg_rows, us=2.0,
        )
        if layer > 0:
            out_weight = fetched(f"out_{layer}", *out_place[layer])
        parts = summed_rows([attn, gated], out_weight)
        if layer > 0:
            parts, gate_up_weight = together(parts, fetched(f"gate_up_{layer}", *gate_up_place[layer]))
        parts, (rows,) = together(parts, restored(f"hidden_{layer}", [hidden]))
        hidden1, normed2, inverse2 = add_norm(rows, parts, gains[layer, 1])
        if layer > 0:
            normed_parts, down_weight = from_all(normed2, fetched("down_1", *down_place[layer]))
        else:
            normed_parts = from_all(normed2)
            gate_up_weight, down_weight = fetched_all("ffn_0", [gate_up_place[layer], down_place[layer]])
        wide_kept = kept((ROWS, 512))
        normed2_b, gate, up, act_b, act_kept = run_kernel(
            gate_up_kernel, [normed_kept, wide_kept, wide_kept, shape_of((ROWS, 512), bf16), kept((ROWS, 512), bf16)],
            None, *passed(normed_parts), gate_up_weight, us=2.3,
        )
        saved.append(
            (
                hidden, normed_b, inverse1, shared_ext, shared_kept, query_kept, x_ext, xc_kept, z_kept, dtn_kept,
                rates_kept, rates_t_kept, pairs, log_total, state, ssm_y, attn_kept, gated_kept, hidden1, inverse2, normed2_b,
                gate, up, act_kept,
            )
        )
        if layer + 1 < layers:
            parts, (rows,) = together(summed_rows([act_b], down_weight), restored(f"hidden1_{layer}", [hidden1]))
            hidden, next_normed, inverse1 = add_norm(rows, parts, gains[layer + 1, 0])
            normed_parts, proj_weight = from_all(next_normed, fetched("proj_1", *proj_place[layer + 1]))

    small_parts = [None] * layers
    inner = None
    for layer in reversed(range(layers)):
        (
            hidden, normed_b, inverse1, shared_ext, shared, query, x_ext, xc, z, dtn, rates, rates_t,
            pairs, log_total, state, ssm_y, attn, gated, hidden1, inverse2, normed2_b, gate, up, act_b,
        ) = saved[layer]
        last = layer == 0
        dffn_b, dgate_up = run_kernel(
            gate_up_back_kernel, [normed_kept, shape_of((ROWS, 1024), bf16)],
            None, *passed(dffn_parts), down_weight, stored(gate), stored(up), us=2.7,
        )
        parts = summed_rows([dgate_up], gate_up_weight)
        outer = weight_gradients(
            [(normed2_b, dgate_up), (dffn_b, act_b)], 3072 if last else 2560, 1536, 0, inner
        )
        parts, outer = lax.optimization_barrier((parts, outer))
        parts, kept_rows = together(parts, restored(f"norm2_{layer}", [grad_hidden, hidden1, inverse2]))
        grad_mid, dmix, ggain2 = norm_back(parts, *kept_rows, gains[layer, 1])
        dmix_parts = from_all(dmix)
        dmix_parts, fetch = from_all(
            dmix,
            fetched_all(
                f"mixer_{layer}",
                [out_place[layer]]
                + [(array, 0, array.shape[1]) for array in (z, ssm_y, shared, rates, rates_t, xc, query, pairs, state)],
            ),
        )
        from_kept = [stored(array) for array in (shared, xc, rates, rates_t, state)]
        out_weight, z, ssm_y, shared, rates, rates_t, xc, query, pairs, state = fetch
        dmix_b, dattn, dy, dz, message = run_kernel(
            gate_back_kernel,
            [
                normed_kept, shape_of((ROWS, HD), bf16), shape_of((ROWS, XLOC)), shape_of((ROWS, XLOC), bf16),
                shape_of((MSG, NSTATE), bf16),
            ],
            flags, *passed(dmix_parts), out_weight, z, ssm_y, shared, rates, rates_t, table, us=2.6,
            scratch=[pltpu.VMEM((ROWS, XLOC), f32), pltpu.VMEM((ROWS, 512), f32)],
        )
        after = tuple(along_ctx(message, -ahead) for ahead in (1, 2, 3))
        early, mine, theirs = run_kernel(
            attention_back_kernel,
            [kept((ROWS, 512), bf16), shape_of((4 * ROWS, HD)), shape_of((4 * ROWS, HD), bf16)],
            flags, dattn, dz, query, pairs, stored(log_total), table, seg_rows, us=2.9,
        )
        got = other_core(theirs)
        dx, dshared, drates, dskip = run_kernel(
            intra_back_kernel,
            [kept((ROWS, XLOC)), kept((ROWS, 2 * NSTATE)), kept((ROWS, 256)), kept((1, XLOC))],
            flags, dy, xc, shared, rates, rates_t, table, seg_rows, state, small[layer], us=3.6,
            scratch=[pltpu.VMEM((128, ROWS), f32), pltpu.VMEM((ROWS, 128), f32)],
        )
        dkv = parts_from(mine, got, along_ctx, -1)
        width = outer.shape[1]
        outer = weight_gradients([(dmix_b, attn), (dmix_b, gated)], width, 512, 3, outer)
        outer = weight_gradients([(normed_b, early)], width, 512, 4, outer)
        if last:
            after, dkv, outer, dx, upper = together(after, dkv, outer, dx, upper)
            lower = lax.psum_scatter(outer, ("fsdp", "ctx"), scatter_dimension=0, tiled=True)
        else:
            after, dkv, outer, dx = together(after, dkv, outer, dx)
            upper = lax.psum_scatter(outer, ("fsdp", "ctx"), scatter_dimension=0, tiled=True)
        packed_grads, state_grad = run_kernel(
            packed_back_kernel, [shape_of((8 * ROWS, 128), bf16), kept((XLOC, NSTATE))],
            flags, *map(stored, after), *from_kept[:3], table, stored(dshared), *map(stored, dkv), us=2.5,
        )
        dshared_parts = parts_of_sum(packed_grads[: 4 * ROWS], packed_grads[4 * ROWS :], along_y, 1)
        dxpre, edge_x, gconv_x, ddt, gheads = run_kernel(
            state_back_kernel,
            [kept((ROWS, XLOC)), shape_of((8, XLOC)), kept((8, XLOC)), kept((ROWS, 128)), kept((8, 128))],
            flags, stored(state_grad), *from_kept[:4], table, from_kept[4], stored(small[layer]),
            stored(dtn), stored(dx), stored(drates), stored(x_ext),
            scratch=[pltpu.VMEM((272, XLOC), f32), pltpu.VMEM((ROWS, XLOC), f32), pltpu.VMEM((ROWS, 128), f32)],
            us=3.5,
        )
        dshared_parts, edge_x = together(dshared_parts, edge_x)
        edge_x = along_ctx(edge_x, -1)
        dsh, edge_sh, gconv_sh = run_kernel(
            shared_back_kernel,
            [shape_of((ROWS, 128)), shape_of((8, 128)), kept((8, 128))],
            flags, *summands(dshared_parts), stored(shared_ext), table, small[layer],
            scratch=[pltpu.VMEM((272, 128), f32)],
        )
        edge_sh, proj_weight = together(
            along_ctx(edge_sh, -1), fetched(f"proj_again_{layer}", *proj_place[layer])
        )
        (late,) = run_kernel(
            late_kernel, [shape_of((ROWS, LATE), bf16)], flags, stored(dxpre), Columns(edge_x), dsh,
            Columns(edge_sh), stored(ddt),
        )
        parts = summed_rows([early, late], proj_weight)
        if not last:
            inner = weight_gradients([(normed_b, Columns(late, 0, 512))], 3072, 512, 5)
            parts, inner = together(parts, inner)
            upper_pair = (normed_b, Columns(late, 4, 128))
        else:
            parts, owned = together(parts, owned_gradients([(normed_b, late), upper_pair]))
        parts, kept_rows = together(parts, restored(f"norm1_{layer}", [grad_mid, hidden, inverse1]))
        grad_hidden, rounded, ggain1 = norm_back(parts, *kept_rows, gains[layer, 0])
        if last:
            dffn_parts = from_all(rounded)
        else:
            dffn_parts, (down_weight, gate_up_weight) = from_all(
                rounded, fetched_all("ffn_again", [down_place[layer - 1], gate_up_place[layer - 1]])
            )
            last_hidden1, last_act = hidden1, act_b
        (small_parts[layer],) = run_kernel(
            small_kernel, [shape_of((64, 128), bf16)],
            None, *map(stored, (ggain1, ggain2, gconv_sh, gconv_x, gheads, dskip)),
        )
    (small_all,) = run_kernel(
        spread_kernel, [shape_of((128, 128), bf16)], None, jnp.concatenate(small_parts, axis=0),
        scratch=[pltpu.VMEM((128, 128), f32)],
    )
    owned = lax.all_to_all(with_small(owned, small_all), ("fsdp", "ctx"), 0, 0, tiled=True)
    (input_grad,) = run_kernel(natural_kernel, [kept((ROWS, model))], flags, *passed(dffn_parts))
    last_act, down_weight, _ = together(last_act, fetched("down_last", *down_place[1]), small_parts[0])
    (layer_out,) = run_kernel(
        output_kernel, [shape_of((SHARE, model), bf16)], None,
        stored(last_hidden1), *summands(summed_rows([last_act], down_weight)),
    )
    (layer_out,) = run_kernel(natural_kernel, [normed_kept], flags, *passed(from_all(layer_out)))
    def pair_of(width):
        return shape_of((layers, model // 16, width))

    owned, layer_out, input_grad = together(owned, layer_out, input_grad)
    over_tp, late_sum, gconv_x, gheads = run_kernel(
        block_sum_kernel,
        [
            shape_of((352, 128), bf16), kept((model // 16, LATE)), shape_of((layers * (CONV + 1), XLOC)),
            shape_of((8, 128)),
        ],
        None, Columns(owned),
        scratch=[pltpu.VMEM((128, 128), f32)],
    )
    grad_shared, ggains1, ggains2, gconv_bc = run_kernel(
        tp_outputs_kernel,
        [
            pair_of(1024), shape_of((layers, model)), shape_of((layers, model)),
            shape_of((layers * (CONV + 1), 512)),
        ],
        flags, *passed(from_all(over_tp)),
        scratch=[pltpu.VMEM((8, 352, 128), f32)], us=2.0,
    )
    lower, grad_shared = together(lower, grad_shared)
    grad_attn, grad_ssm, grad_gate, grad_up, grad_down, grad_query, grad_zx, grad_dt = run_kernel(
        weight_outputs_kernel,
        [
            *(kept((layers, model // 16, width)) for width in (128, 384, 512, 512, 512, 128)),
            shape_of((layers, model // 16, 2, XLOC)), pair_of(HLOC),
        ],
        None, stored(lower), stored(upper), stored(late_sum), us=3.0,
    )
    gconv_x = gconv_x.reshape(layers, CONV + 1, XLOC)
    gconv_bc = gconv_bc.reshape(layers, CONV + 1, 512)
    gheads = gheads[: 3 * layers].reshape(layers, 3, 128)[:, :, :HLOC]
    return (
        layer_out[None],
        input_grad[None],
        grad_query,
        grad_shared,
        grad_zx,
        grad_dt,
        grad_attn,
        grad_ssm,
        grad_gate,
        grad_up,
        grad_down,
        ggains1,
        gconv_x,
        gconv_bc,
        gheads[:, :2],
        ggains2,
        gheads[:, 2],
    )


def solution(mesh):
    columns = P(None, ("fsdp", "ctx"), "tp")
    rows = P("fsdp", "ctx", None)
    return jax.shard_map(
        body,
        mesh=mesh,
        in_specs=(
            rows, rows, P("fsdp", None), columns, P(None, ("fsdp", "ctx"), None),
            P(None, ("fsdp", "ctx"), None, "tp"), columns, columns, columns, columns, columns, columns,
            P(), P(None, None, "tp"), P(), P(None, None, "tp"),
        ),
        out_specs=(
            rows, rows, columns, P(None, ("fsdp", "ctx"), None), P(None, ("fsdp", "ctx"), None, "tp"),
            columns, columns, columns, columns, columns, columns,
            P(), P(None, None, "tp"), P(), P(None, None, "tp"), P(), P(None, "tp"),
        ),
        check_vma=False,
    )
```

profile of v0, /device:TPU:1, one launch (start us, length us, event | category | flops | bytes accessed | tf_op | source)
XLA Modules:
  0.0 602.5 jit_solution(3226973170775659936)
XLA Ops:
  25.6 52.7 %all-gather.4.cloned.1.call-done.weight.refs_0_ = bf16[2048,1664]{1,0:T(8,128)(2,1)} async-done(((bf16[128,1664]{1,0:T(8,128)(2,1)}), bf16[2048,1664]{1,0:T(8,128)(2,1)}) %all-gather.4.cloned.1.call-update) | async-done | bytes 6815760 | tf_op jit(solution)/shard_map/all_gather | solution.py:1123
  79.5 5.5 shard_map.289
  103.7 3.9 collective-permute-start.8
  107.7 4.3 collective-permute-start.9
  116.1 6.2 %collective-permute-done.9.msg2.h2 = bf16[528,256]{1,0:T(8,128)(2,1)S(1)} collective-permute-done((bf16[528,256]{1,0:T(8,128)(2,1)S(1)}, bf16[528,256]{1,0:T(8,128)(2,1)S(1)}, u32[]{:S(2)}, u32[]{:S(2)}) %collective-permute-start.9) | collective-permute-done | bytes 270368 | tf_op jit(solution)/shard_map/ppermute | solution.py:45
  122.3 5.7 collective-permute-done.10.msg3.h3
  140.6 5.5 collective-permute-done.13.part1
  160.7 6.2 %all-gather.6.cloned.1.call-done.refs_0_.refs_1_ = bf16[2048,2688]{1,0:T(8,128)(2,1)} async-done(((bf16[128,2688]{1,0:T(8,128)(2,1)}), bf16[2048,2688]{1,0:T(8,128)(2,1)}) %all-gather.6.cloned.1.call-update) | async-done | bytes 11010064 | tf_op jit(solution)/shard_map/all_gather | solution.py:1123
  180.3 4.8 collective-permute-done.24.part1
  187.1 3.4 collective-permute-start.27
  201.4 3.4 shard_map.305
  220.2 4.1 collective-permute-start.42
  224.3 7.1 %collective-permute-start.43 = (bf16[528,256]{1,0:T(8,128)(2,1)S(1)}, bf16[528,256]{1,0:T(8,128)(2,1)S(1)}, u32[]{:S(2)}, u32[]{:S(2)}) collective-permute-start(bf16[528,256]{1,0:T(8,128)(2,1)S(1)} %get-tuple-element.526), channel_id=1, source_target_pairs={{0,16},{8,24},{1,17},{9,25},{2,18},{10,26},{3,19},{11,27},{4,20},{... | collective-permute-start | bytes 811016 | tf_op jit(solution)/shard_map/ppermute | solution.py:45
  236.1 10.4 %collective-permute-done.43.msg2.h2 = bf16[528,256]{1,0:T(8,128)(2,1)S(1)} collective-permute-done((bf16[528,256]{1,0:T(8,128)(2,1)S(1)}, bf16[528,256]{1,0:T(8,128)(2,1)S(1)}, u32[]{:S(2)}, u32[]{:S(2)}) %collective-permute-start.43) | collective-permute-done | bytes 270368 | tf_op jit(solution)/shard_map/ppermute | solution.py:45
  294.7 4.4 shard_map.321.refs_4_
  326.5 3.7 shard_map.328
  334.8 3.1 shard_map.326.refs_2_
  352.8 4.6 shard_map.330
  388.6 3.3 ffn_again.1
  409.4 4.4 shard_map.341.refs_4_
  417.3 3.4 collective-permute-start.96
  441.6 3.6 shard_map.348
  449.9 3.1 shard_map.346.refs_2_
  456.9 3.6 collective-permute-done.109.kv3
  468.6 4.4 shard_map.350
  496.0 4.9 shard_map.356.block
  506.5 7.4 %all-to-all-start = ((bf16[16,128,768]{2,1,0:T(8,128)(2,1)}), bf16[16,128,768]{2,1,0:T(8,128)(2,1)S(1)}, u32[]{:S(2)}, u32[]{:S(2)}) async-start(bf16[16,128,768]{2,1,0:T(8,128)(2,1)} %shard_map.361), calls=%async_computation.1 | async-start | bytes 6291456 | tf_op jit(solution)/shard_map/all_to_all | solution.py:1355
  520.9 3.8 collective-permute-start.122
  538.9 3.7 collective-permute-start.128
  549.7 19.2 %all-to-all-done.values = bf16[16,128,768]{2,1,0:T(8,128)(2,1)S(1)} async-done(((bf16[16,128,768]{2,1,0:T(8,128)(2,1)}), bf16[16,128,768]{2,1,0:T(8,128)(2,1)S(1)}, u32[]{:S(2)}, u32[]{:S(2)}) %all-to-all-start) | async-done | bytes 3145760 | tf_op jit(solution)/shard_map/all_to_all | solution.py:1355
  584.8 6.9 %reduce-scatter.5.cloned.1.call-done.lower = bf16[128,3072]{1,0:T(8,128)(2,1)} async-done(((bf16[2048,3072]{1,0:T(8,128)(2,1)}), bf16[128,3072]{1,0:T(8,128)(2,1)}) %reduce-scatter.5.cloned.1.call-update) | async-done | bytes 786448 | tf_op jit(solution)/shard_map/reduce_scatter | solution.py:1299
  591.7 3.1 shard_map.369
  (502 shorter events, 373.1 us)
Async XLA Ops:
  7.2 71.1 %all-gather.4.cloned.1.call-start = ((), (), s32[]{:S(2)}) async-start(), calls=%async_computation.3 | async-start | bytes 7241728 | tf_op jit(solution)/shard_map/all_gather | solution.py:1123
  11.1 155.8 %all-gather.6.cloned.1.call-start = ((), (), s32[]{:S(2)}) async-start(), calls=%async_computation.4 | async-start | bytes 11698176 | tf_op jit(solution)/shard_map/all_gather | solution.py:1123
  13.7 233.5 %all-gather.8.cloned.1.call-start = ((), (), s32[]{:S(2)}) async-start(), calls=%async_computation.5 | async-start | bytes 8912896 | tf_op jit(solution)/shard_map/all_gather | solution.py:1123
  15.8 444.8 %reduce-scatter.3.cloned.1.call-start = ((), (), s32[]{:S(2)}) async-start(), calls=%async_computation.6 | async-start | bytes 11141120 | tf_op jit(solution)/shard_map/reduce_scatter | solution.py:1302
  103.7 12.4 %collective-permute-start.8 = (bf16[528,256]{1,0:T(8,128)(2,1)S(1)}, bf16[528,256]{1,0:T(8,128)(2,1)S(1)}, u32[]{:S(2)}, u32[]{:S(2)}) collective-permute-start(bf16[528,256]{1,0:T(8,128)(2,1)S(1)} %get-tuple-element.466), channel_id=1, source_target_pairs={{0,8},{8,16},{16,24},{1,9},{9,17},{17,25},{2,10},{10,18},{18,26},{... | collective-permute-start | bytes 811016 | tf_op jit(solution)/shard_map/ppermute | solution.py:45
  107.7 14.7 %collective-permute-start.9 = (bf16[528,256]{1,0:T(8,128)(2,1)S(1)}, bf16[528,256]{1,0:T(8,128)(2,1)S(1)}, u32[]{:S(2)}, u32[]{:S(2)}) collective-permute-start(bf16[528,256]{1,0:T(8,128)(2,1)S(1)} %get-tuple-element.466), channel_id=1, source_target_pairs={{0,16},{8,24},{1,17},{9,25},{2,18},{10,26},{3,19},{11,27},{4,20},{... | collective-permute-start | bytes 811016 | tf_op jit(solution)/shard_map/ppermute | solution.py:45
  112.0 16.1 %collective-permute-start.10 = (bf16[528,256]{1,0:T(8,128)(2,1)S(1)}, bf16[528,256]{1,0:T(8,128)(2,1)S(1)}, u32[]{:S(2)}, u32[]{:S(2)}) collective-permute-start(bf16[528,256]{1,0:T(8,128)(2,1)S(1)} %get-tuple-element.466), channel_id=1, source_target_pairs={{0,24},{1,25},{2,26},{3,27},{4,28},{5,29},{6,30},{7,31},{32,56},{3... | collective-permute-start | bytes 811016 | tf_op jit(solution)/shard_map/ppermute | solution.py:45
  151.4 18.3 %collective-permute-start.19 = (bf16[32,2048]{1,0:T(8,128)(2,1)S(1)}, bf16[32,2048]{1,0:T(8,128)(2,1)S(1)}, u32[]{:S(2)}, u32[]{:S(2)}) collective-permute-start(bf16[32,2048]{1,0:T(8,128)(2,1)S(1)} %get-tuple-element.490.p0), channel_id=1, source_target_pairs={{0,1},{1,0},{2,3},{3,2},{4,5},{5,4},{6,7},{7,6},{8,9},{9,8},{10,11... | collective-permute-start | bytes 393224 | tf_op jit(solution)/shard_map/ppermute | solution.py:40
  154.4 15.4 %collective-permute-start.20 = (bf16[32,2048]{1,0:T(8,128)(2,1)S(1)}, bf16[32,2048]{1,0:T(8,128)(2,1)S(1)}, u32[]{:S(2)}, u32[]{:S(2)}) collective-permute-start(bf16[32,2048]{1,0:T(8,128)(2,1)S(1)} %collective-permute-done.16.p1), channel_id=1, source_target_pairs={{0,1},{1,0},{2,3},{3,2},{4,5},{5,4},{6,7},{7,6},{8,9},{9,8},{10,11... | collective-permute-start | bytes 393224 | tf_op jit(solution)/shard_map/ppermute | solution.py:40
  157.3 12.5 %collective-permute-start.21 = (bf16[32,2048]{1,0:T(8,128)(2,1)S(1)}, bf16[32,2048]{1,0:T(8,128)(2,1)S(1)}, u32[]{:S(2)}, u32[]{:S(2)}) collective-permute-start(bf16[32,2048]{1,0:T(8,128)(2,1)S(1)} %collective-permute-done.17.p2), channel_id=1, source_target_pairs={{0,1},{1,0},{2,3},{3,2},{4,5},{5,4},{6,7},{7,6},{8,9},{9,8},{10,11... | collective-permute-start | bytes 393224 | tf_op jit(solution)/shard_map/ppermute | solution.py:40
  159.9 9.8 %collective-permute-start.22 = (bf16[32,2048]{1,0:T(8,128)(2,1)S(1)}, bf16[32,2048]{1,0:T(8,128)(2,1)S(1)}, u32[]{:S(2)}, u32[]{:S(2)}) collective-permute-start(bf16[32,2048]{1,0:T(8,128)(2,1)S(1)} %collective-permute-done.18.p3), channel_id=1, source_target_pairs={{0,1},{1,0},{2,3},{3,2},{4,5},{5,4},{6,7},{7,6},{8,9},{9,8},{10,11... | collective-permute-start | bytes 393224 | tf_op jit(solution)/shard_map/ppermute | solution.py:40
  220.2 15.9 %collective-permute-start.42 = (bf16[528,256]{1,0:T(8,128)(2,1)S(1)}, bf16[528,256]{1,0:T(8,128)(2,1)S(1)}, u32[]{:S(2)}, u32[]{:S(2)}) collective-permute-start(bf16[528,256]{1,0:T(8,128)(2,1)S(1)} %get-tuple-element.526), channel_id=1, source_target_pairs={{0,8},{8,16},{16,24},{1,9},{9,17},{17,25},{2,10},{10,18},{18,26},{... | collective-permute-start | bytes 811016 | tf_op jit(solution)/shard_map/ppermute | solution.py:45
  224.3 22.1 %collective-permute-start.43 = (bf16[528,256]{1,0:T(8,128)(2,1)S(1)}, bf16[528,256]{1,0:T(8,128)(2,1)S(1)}, u32[]{:S(2)}, u32[]{:S(2)}) collective-permute-start(bf16[528,256]{1,0:T(8,128)(2,1)S(1)} %get-tuple-element.526), channel_id=1, source_target_pairs={{0,16},{8,24},{1,17},{9,25},{2,18},{10,26},{3,19},{11,27},{4,20},{... | collective-permute-start | bytes 811016 | tf_op jit(solution)/shard_map/ppermute | solution.py:45
  231.4 15.0 %collective-permute-start.44 = (bf16[528,256]{1,0:T(8,128)(2,1)S(1)}, bf16[528,256]{1,0:T(8,128)(2,1)S(1)}, u32[]{:S(2)}, u32[]{:S(2)}) collective-permute-start(bf16[528,256]{1,0:T(8,128)(2,1)S(1)} %get-tuple-element.526), channel_id=1, source_target_pairs={{0,24},{1,25},{2,26},{3,27},{4,28},{5,29},{6,30},{7,31},{32,56},{3... | collective-permute-start | bytes 811016 | tf_op jit(solution)/shard_map/ppermute | solution.py:45
  319.4 14.1 %collective-permute-start.68 = (bf16[400,256]{1,0:T(8,128)(2,1)}, bf16[400,256]{1,0:T(8,128)(2,1)S(1)}, u32[]{:S(2)}, u32[]{:S(2)}) collective-permute-start(bf16[400,256]{1,0:T(8,128)(2,1)} %get-tuple-element.618), channel_id=1, source_target_pairs={{8,0},{16,8},{24,16},{9,1},{17,9},{25,17},{10,2},{18,10},{26,18},{... | collective-permute-start | bytes 614408 | tf_op jit(solution)/shard_map/ppermute | solution.py:45
  320.7 20.1 %collective-permute-start.69 = (bf16[400,256]{1,0:T(8,128)(2,1)}, bf16[400,256]{1,0:T(8,128)(2,1)}, u32[]{:S(2)}, u32[]{:S(2)}) collective-permute-start(bf16[400,256]{1,0:T(8,128)(2,1)} %get-tuple-element.618), channel_id=1, source_target_pairs={{16,0},{24,8},{17,1},{25,9},{18,2},{26,10},{19,3},{27,11},{20,4},{... | collective-permute-start | bytes 614408 | tf_op jit(solution)/shard_map/ppermute | solution.py:45
  322.0 18.8 %collective-permute-start.70 = (bf16[400,256]{1,0:T(8,128)(2,1)}, bf16[400,256]{1,0:T(8,128)(2,1)}, u32[]{:S(2)}, u32[]{:S(2)}) collective-permute-start(bf16[400,256]{1,0:T(8,128)(2,1)} %get-tuple-element.618), channel_id=1, source_target_pairs={{24,0},{25,1},{26,2},{27,3},{28,4},{29,5},{30,6},{31,7},{56,32},{5... | collective-permute-start | bytes 614408 | tf_op jit(solution)/shard_map/ppermute | solution.py:45
  330.9 9.9 %collective-permute-start.72 = (bf16[256,128]{1,0:T(8,128)(2,1)S(1)}, bf16[256,128]{1,0:T(8,128)(2,1)S(1)}, u32[]{:S(2)}, u32[]{:S(2)}) collective-permute-start(bf16[256,128]{1,0:T(8,128)(2,1)S(1)} %get-tuple-element.622), channel_id=1, source_target_pairs={{8,0},{16,8},{24,16},{9,1},{17,9},{25,17},{10,2},{18,10},{26,18},{... | collective-permute-start | bytes 196616 | tf_op jit(solution)/shard_map/ppermute | solution.py:45
  333.5 10.7 %collective-permute-start.74 = (bf16[256,128]{1,0:T(8,128)(2,1)S(1)}, bf16[256,128]{1,0:T(8,128)(2,1)S(1)}, u32[]{:S(2)}, u32[]{:S(2)}) collective-permute-start(bf16[256,128]{1,0:T(8,128)(2,1)S(1)} %get-tuple-element.624), channel_id=1, source_target_pairs={{24,0},{25,1},{26,2},{27,3},{28,4},{29,5},{30,6},{31,7},{56,32},{5... | collective-permute-start | bytes 196616 | tf_op jit(solution)/shard_map/ppermute | solution.py:45
  344.9 246.9 %reduce-scatter.5.cloned.1.call-start = ((), (), s32[]{:S(2)}) async-start(), calls=%async_computation.7 | async-start | bytes 13369344 | tf_op jit(solution)/shard_map/reduce_scatter | solution.py:1299
  434.3 14.3 %collective-permute-start.103 = (bf16[400,256]{1,0:T(8,128)(2,1)}, bf16[400,256]{1,0:T(8,128)(2,1)S(1)}, u32[]{:S(2)}, u32[]{:S(2)}) collective-permute-start(bf16[400,256]{1,0:T(8,128)(2,1)} %get-tuple-element.755), channel_id=1, source_target_pairs={{8,0},{16,8},{24,16},{9,1},{17,9},{25,17},{10,2},{18,10},{26,18},{... | collective-permute-start | bytes 614408 | tf_op jit(solution)/shard_map/ppermute | solution.py:45
  435.6 20.3 %collective-permute-start.104 = (bf16[400,256]{1,0:T(8,128)(2,1)}, bf16[400,256]{1,0:T(8,128)(2,1)}, u32[]{:S(2)}, u32[]{:S(2)}) collective-permute-start(bf16[400,256]{1,0:T(8,128)(2,1)} %get-tuple-element.755), channel_id=1, source_target_pairs={{16,0},{24,8},{17,1},{25,9},{18,2},{26,10},{19,3},{27,11},{20,4},{... | collective-permute-start | bytes 614408 | tf_op jit(solution)/shard_map/ppermute | solution.py:45
  436.9 19.0 %collective-permute-start.105 = (bf16[400,256]{1,0:T(8,128)(2,1)}, bf16[400,256]{1,0:T(8,128)(2,1)}, u32[]{:S(2)}, u32[]{:S(2)}) collective-permute-start(bf16[400,256]{1,0:T(8,128)(2,1)} %get-tuple-element.755), channel_id=1, source_target_pairs={{24,0},{25,1},{26,2},{27,3},{28,4},{29,5},{30,6},{31,7},{56,32},{5... | collective-permute-start | bytes 614408 | tf_op jit(solution)/shard_map/ppermute | solution.py:45
  445.9 9.9 %collective-permute-start.107 = (bf16[256,128]{1,0:T(8,128)(2,1)}, bf16[256,128]{1,0:T(8,128)(2,1)}, u32[]{:S(2)}, u32[]{:S(2)}) collective-permute-start(bf16[256,128]{1,0:T(8,128)(2,1)} %get-tuple-element.759), channel_id=1, source_target_pairs={{8,0},{16,8},{24,16},{9,1},{17,9},{25,17},{10,2},{18,10},{26,18},{... | collective-permute-start | bytes 196616 | tf_op jit(solution)/shard_map/ppermute | solution.py:45
  447.2 9.7 %collective-permute-start.108 = (bf16[256,128]{1,0:T(8,128)(2,1)}, bf16[256,128]{1,0:T(8,128)(2,1)}, u32[]{:S(2)}, u32[]{:S(2)}) collective-permute-start(bf16[256,128]{1,0:T(8,128)(2,1)} %get-tuple-element.760), channel_id=1, source_target_pairs={{16,0},{24,8},{17,1},{25,9},{18,2},{26,10},{19,3},{27,11},{20,4},{... | collective-permute-start | bytes 196616 | tf_op jit(solution)/shard_map/ppermute | solution.py:45
  448.6 12.0 %collective-permute-start.109 = (bf16[256,128]{1,0:T(8,128)(2,1)S(1)}, bf16[256,128]{1,0:T(8,128)(2,1)}, u32[]{:S(2)}, u32[]{:S(2)}) collective-permute-start(bf16[256,128]{1,0:T(8,128)(2,1)S(1)} %get-tuple-element.761), channel_id=1, source_target_pairs={{24,0},{25,1},{26,2},{27,3},{28,4},{29,5},{30,6},{31,7},{56,32},{5... | collective-permute-start | bytes 196616 | tf_op jit(solution)/shard_map/ppermute | solution.py:45
  489.5 11.5 %collective-permute-start.117 = (bf16[32,2048]{1,0:T(8,128)(2,1)S(1)}, bf16[32,2048]{1,0:T(8,128)(2,1)S(1)}, u32[]{:S(2)}, u32[]{:S(2)}) collective-permute-start(bf16[32,2048]{1,0:T(8,128)(2,1)S(1)} %get-tuple-element.805), channel_id=1, source_target_pairs={{0,2},{1,3},{2,4},{3,5},{4,6},{5,7},{6,0},{7,1},{8,10},{9,11},{10,... | collective-permute-start | bytes 393224 | tf_op jit(solution)/shard_map/ppermute | solution.py:36
  489.9 11.0 %collective-permute-start.118 = (bf16[32,2048]{1,0:T(8,128)(2,1)S(1)}, bf16[32,2048]{1,0:T(8,128)(2,1)S(1)}, u32[]{:S(2)}, u32[]{:S(2)}) collective-permute-start(bf16[32,2048]{1,0:T(8,128)(2,1)S(1)} %get-tuple-element.806), channel_id=1, source_target_pairs={{0,4},{1,5},{2,6},{3,7},{4,0},{5,1},{6,2},{7,3},{8,12},{9,13},{10,... | collective-permute-start | bytes 393224 | tf_op jit(solution)/shard_map/ppermute | solution.py:36
  506.5 62.4 %all-to-all-start = ((bf16[16,128,768]{2,1,0:T(8,128)(2,1)}), bf16[16,128,768]{2,1,0:T(8,128)(2,1)S(1)}, u32[]{:S(2)}, u32[]{:S(2)}) async-start(bf16[16,128,768]{2,1,0:T(8,128)(2,1)} %shard_map.361), calls=%async_computation.1 | async-start | bytes 6291456 | tf_op jit(solution)/shard_map/all_to_all | solution.py:1355
  524.7 11.3 %collective-permute-start.133 = (bf16[32,2048]{1,0:T(8,128)(2,1)S(1)}, bf16[32,2048]{1,0:T(8,128)(2,1)S(1)}, u32[]{:S(2)}, u32[]{:S(2)}) collective-permute-start(bf16[32,2048]{1,0:T(8,128)(2,1)S(1)} %copy-done.24), channel_id=1, source_target_pairs={{0,2},{1,3},{2,4},{3,5},{4,6},{5,7},{6,0},{7,1},{8,10},{9,11},{10,... | collective-permute-start | bytes 393224 | tf_op jit(solution)/shard_map/ppermute | solution.py:36
  526.1 10.0 %collective-permute-start.134 = (bf16[32,2048]{1,0:T(8,128)(2,1)S(1)}, bf16[32,2048]{1,0:T(8,128)(2,1)S(1)}, u32[]{:S(2)}, u32[]{:S(2)}) collective-permute-start(bf16[32,2048]{1,0:T(8,128)(2,1)S(1)} %copy-done.24), channel_id=1, source_target_pairs={{0,1},{1,0},{2,3},{3,2},{4,5},{5,4},{6,7},{7,6},{8,9},{9,8},{10,11... | collective-permute-start | bytes 393224 | tf_op jit(solution)/shard_map/ppermute | solution.py:40
  537.7 10.4 %collective-permute-start.127 = (bf16[32,2048]{1,0:T(8,128)(2,1)S(1)}, bf16[32,2048]{1,0:T(8,128)(2,1)S(1)}, u32[]{:S(2)}, u32[]{:S(2)}) collective-permute-start(bf16[32,2048]{1,0:T(8,128)(2,1)S(1)} %shard_map.364.p0), channel_id=1, source_target_pairs={{0,1},{1,0},{2,3},{3,2},{4,5},{5,4},{6,7},{7,6},{8,9},{9,8},{10,11... | collective-permute-start | bytes 393224 | tf_op jit(solution)/shard_map/ppermute | solution.py:40
  (157 other events, 1651.5 us)
Sparse Core Ops, SparseCore 0:
  11.2 67.0 all-gather.3
  81.0 85.8 all-gather.5
  169.0 75.4 all-gather.7
  344.4 89.3 reduce-scatter.2
  460.7 130.9 reduce-scatter.4
where the time goes:
time: 613 us; the launch traced here: 602 us
  starting transfers between devices  204 us (33%)
  Pallas kernels  200 us (33%)
  waiting for transfers between devices  169 us (28%)
  between operations  15.6 us (3%)
  local copies, waits for them, and re-layouts  11.4 us (2%)
    pallas_call x65, Pallas kernels, run_kernel(): pl.pallas_call(kernel, grid=(1,) if any(own) else (), out_shape=tuple(out...  116 us
    ppermute x58, starting transfers between devices, other_core(): return lax.ppermute(value, 'tp', [(i, i ^ 1) for i in range(8)])  79.2 us
    ppermute x63, starting transfers between devices, along_y(): return lax.ppermute(value, 'tp', pairs)  69.4 us
    all_gather x3, waiting for transfers between devices, packed(): return lax.all_gather(columns, ('fsdp', 'ctx'), axis=0, tiled=True)  58.9 us
    ppermute x24, starting transfers between devices, along_ctx(): lax.ppermute(value, 'ctx', [(i, i + steps) for i in range(first, last)])  47.6 us
    ppermute x24, waiting for transfers between devices, along_ctx(): lax.ppermute(value, 'ctx', [(i, i + steps) for i in range(first, last)])  37.7 us
    pallas_call x19, Pallas kernels, fetched_all(): pl.pallas_call(partial(fetch_kernel, places), name=name, out_shape=tuple(...  34.2 us
    ppermute x63, waiting for transfers between devices, along_y(): return lax.ppermute(value, 'tp', pairs)  27.3 us
  transfers between devices with their start and end apart: 151, of which 60 were waited for; matrix products, arithmetic and copies ran while one was open for 1% of the time, Pallas kernels for 29%

commit v1 on v0

--- a/solution.py
+++ b/solution.py
@@ -151,6 +151,29 @@
 
 def restored(name, arrays):
     return fetched_all(name, [(array, 0, array.shape[1]) for array in arrays])
+
+
+def stash_kernel(*refs):
+    count = len(refs) // 2
+    sems = refs[-1]
+    copies = [pltpu.make_async_copy(refs[k], refs[count + k], sems.at[k]) for k in range(count)]
+    for copy in copies:
+        copy.start()
+    for copy in copies:
+        copy.wait()
+
+
+def stashed(name, arrays):
+    return pl.pallas_call(
+        stash_kernel,
+        name=name,
+        out_shape=tuple(pltpu.HBM(array.shape, array.dtype) for array in arrays),
+        in_specs=[pl.BlockSpec(memory_space=pltpu.VMEM)] * len(arrays),
+        out_specs=tuple(pl.BlockSpec(memory_space=pltpu.HBM) for _ in arrays),
+        scratch_shapes=[pltpu.SemaphoreType.DMA((len(arrays),))],
+        compiler_params=pltpu.CompilerParams(vmem_limit_bytes=VMEM_LIMIT),
+        cost_estimate=pl.CostEstimate(flops=10**9, bytes_accessed=10**6, transcendentals=0),
+    )(*arrays)
 
 
 def run_kernel(kernel, outs, flags, *args, scratch=(), us=1.0):
@@ -786,15 +809,14 @@
     return parts_of_sum(own, other, along_y, 1)
 
 
-def gate_up_kernel(p0, p1, p2, p3, p4, p5, p6, p7, weight, normed, gate, up, act, act_kept):
+def gate_up_kernel(p0, p1, p2, p3, p4, p5, p6, p7, weight, normed, gate, up, act):
     rows = joined((p0, p1, p2, p3, p4, p5, p6, p7))
     normed[...] = rows
     result = dot_nn(rows, weight[...])
     g, u = result[:, :512], result[:, 512:]
     gate[...] = g
     up[...] = u
-    for out in (act, act_kept):
-        out[...] = (g * sigmoid(g) * u).astype(bf16)
+    act[...] = (g * sigmoid(g) * u).astype(bf16)
 
 
 def gate_up_back_kernel(*refs):
@@ -830,7 +852,7 @@
     shape = hidden.shape
     return run_kernel(
         add_norm_kernel,
-        [kept(shape), shape_of(shape, bf16), kept((shape[0], 128))],
+        [shape_of(shape), shape_of(shape, bf16), shape_of((shape[0], 128))],
         None, hidden, *summands(parts), gain[None],
     )
 
@@ -857,7 +879,7 @@
     shape = hidden.shape
     return run_kernel(
         norm_back_kernel,
-        [kept(shape), shape_of(shape, bf16), kept((1, shape[1]))],
+        [shape_of(shape), shape_of(shape, bf16), shape_of((1, shape[1]))],
         None, grad, *summands(parts), hidden, inverse, gain[None],
     )
 
@@ -1216,27 +1238,35 @@
             parts, gate_up_weight = together(parts, fetched(f"gate_up_{layer}", *gate_up_place[layer]))
         parts, (rows,) = together(parts, restored(f"hidden_{layer}", [hidden]))
         hidden1, normed2, inverse2 = add_norm(rows, parts, gains[layer, 1])
+        rows = stashed(f"rows_{layer}", [hidden1, inverse2])
         if layer > 0:
-            normed_parts, down_weight = from_all(normed2, fetched("down_1", *down_place[layer]))
+            normed_parts, (down_weight, rows) = from_all(normed2, (fetched("down_1", *down_place[layer]), rows))
         else:
-            normed_parts = from_all(normed2)
+            normed_parts, rows = from_all(normed2, rows)
             gate_up_weight, down_weight = fetched_all("ffn_0", [gate_up_place[layer], down_place[layer]])
-        wide_kept = kept((ROWS, 512))
-        normed2_b, gate, up, act_b, act_kept = run_kernel(
-            gate_up_kernel, [normed_kept, wide_kept, wide_kept, shape_of((ROWS, 512), bf16), kept((ROWS, 512), bf16)],
+        hidden1, inverse2 = rows
+        ffn = run_kernel(
+            gate_up_kernel, [normed_shape, wide, wide, shape_of((ROWS, 512), bf16)],
             None, *passed(normed_parts), gate_up_weight, us=2.3,
         )
+        if layer + 1 < layers:
+            parts = summed_rows([ffn[3]], down_weight)
+            parts, ffn, (rows,) = together(parts, stashed("ffn_kept", ffn), restored(f"hidden1_{layer}", [hidden1]))
+        normed2_b, gate, up, act_b = ffn
         saved.append(
             (
                 hidden, normed_b, inverse1, shared_ext, shared_kept, query_kept, x_ext, xc_kept, z_kept, dtn_kept,
                 rates_kept, rates_t_kept, pairs, log_total, state, ssm_y, attn_kept, gated_kept, hidden1, inverse2, normed2_b,
-                gate, up, act_kept,
+                gate, up, act_b,
             )
         )
         if layer + 1 < layers:
-            parts, (rows,) = together(summed_rows([act_b], down_weight), restored(f"hidden1_{layer}", [hidden1]))
             hidden, next_normed, inverse1 = add_norm(rows, parts, gains[layer + 1, 0])
-            normed_parts, proj_weight = from_all(next_normed, fetched("proj_1", *proj_place[layer + 1]))
+            normed_parts, (proj_weight, rows) = from_all(
+                next_normed,
+                (fetched("proj_1", *proj_place[layer + 1]), stashed("rows_next", [hidden, inverse1])),
+            )
+            hidden, inverse1 = rows
 
     small_parts = [None] * layers
     inner = None
@@ -1247,8 +1277,8 @@
         ) = saved[layer]
         last = layer == 0
         dffn_b, dgate_up = run_kernel(
-            gate_up_back_kernel, [normed_kept, shape_of((ROWS, 1024), bf16)],
-            None, *passed(dffn_parts), down_weight, stored(gate), stored(up), us=2.7,
+            gate_up_back_kernel, [normed_shape, shape_of((ROWS, 1024), bf16)],
+            None, *passed(dffn_parts), down_weight, *(map(stored, (gate, up)) if last else (gate, up)), us=2.7,
         )
         parts = summed_rows([dgate_up], gate_up_weight)
         outer = weight_gradients(
@@ -1258,14 +1288,24 @@
         parts, kept_rows = together(parts, restored(f"norm2_{layer}", [grad_hidden, hidden1, inverse2]))
         grad_mid, dmix, ggain2 = norm_back(parts, *kept_rows, gains[layer, 1])
         dmix_parts = from_all(dmix)
-        dmix_parts, fetch = from_all(
+        beside = [grad_mid, ggain2] if last else [grad_mid, ggain2, act_b]
+        dmix_parts, (fetch, rows) = from_all(
             dmix,
-            fetched_all(
-                f"mixer_{layer}",
-                [out_place[layer]]
-                + [(array, 0, array.shape[1]) for array in (z, ssm_y, shared, rates, rates_t, xc, query, pairs, state)],
+            (
+                fetched_all(
+                    f"mixer_{layer}",
+                    [out_place[layer]]
+                    + [
+                        (array, 0, array.shape[1])
+                        for array in (z, ssm_y, shared, rates, rates_t, xc, query, pairs, state)
+                    ],
+                ),
+                stashed(f"grads_{layer}", beside),
             ),
         )
+        grad_mid, ggain2 = rows[:2]
+        if not last:
+            last_act = rows[2]
         from_kept = [stored(array) for array in (shared, xc, rates, rates_t, state)]
         out_weight, z, ssm_y, shared, rates, rates_t, xc, query, pairs, state = fetch
         dmix_b, dattn, dy, dz, message = run_kernel(
@@ -1340,13 +1380,17 @@
         if last:
             dffn_parts = from_all(rounded)
         else:
-            dffn_parts, (down_weight, gate_up_weight) = from_all(
-                rounded, fetched_all("ffn_again", [down_place[layer - 1], gate_up_place[layer - 1]])
+            dffn_parts, ((down_weight, gate_up_weight), (grad_hidden, ggain1)) = from_all(
+                rounded,
+                (
+                    fetched_all("ffn_again", [down_place[layer - 1], gate_up_place[layer - 1]]),
+                    stashed("grads_next", [grad_hidden, ggain1]),
+                ),
             )
-            last_hidden1, last_act = hidden1, act_b
+            last_hidden1 = hidden1
         (small_parts[layer],) = run_kernel(
             small_kernel, [shape_of((64, 128), bf16)],
-            None, *map(stored, (ggain1, ggain2, gconv_sh, gconv_x, gheads, dskip)),
+            None, ggain1, *map(stored, (ggain2, gconv_sh, gconv_x, gheads, dskip)),
         )
     (small_all,) = run_kernel(
         spread_kernel, [shape_of((128, 128), bf16)], None, jnp.concatenate(small_parts, axis=0),

time: 613 us -> 606 us (0.989)
    pallas_call x65, Pallas kernels: 116 us -> 107 us  [run_kernel(): pl.pallas_call(kernel, grid=(1,) if any(own) else (), out_shape=tuple(out...]
  transfers between devices with their start and end apart: 151 -> 151, of which waited for: 60 -> 59; matrix products, arithmetic and copies ran while one was open for 1% -> 1% of each run, Pallas kernels for 29% -> 30%
where the time goes in v1:
time: 606 us; the launch traced here: 596 us
  starting transfers between devices  204 us (34%)
  Pallas kernels  197 us (33%)
  waiting for transfers between devices  167 us (28%)
  between operations  15.5 us (3%)
  local copies, waits for them, and re-layouts  9.57 us (2%)
    pallas_call x65, Pallas kernels, run_kernel(): pl.pallas_call(kernel, grid=(1,) if any(own) else (), out_shape=tuple(out...  107 us
    ppermute x58, starting transfers between devices, other_core(): return lax.ppermute(value, 'tp', [(i, i ^ 1) for i in range(8)])  76.8 us
    ppermute x63, starting transfers between devices, along_y(): return lax.ppermute(value, 'tp', pairs)  72.2 us
    all_gather x3, waiting for transfers between devices, packed(): return lax.all_gather(columns, ('fsdp', 'ctx'), axis=0, tiled=True)  60.6 us
    ppermute x24, starting transfers between devices, along_ctx(): lax.ppermute(value, 'ctx', [(i, i + steps) for i in range(first, last)])  47.8 us
    ppermute x24, waiting for transfers between devices, along_ctx(): lax.ppermute(value, 'ctx', [(i, i + steps) for i in range(first, last)])  38.7 us
    pallas_call x19, Pallas kernels, fetched_all(): pl.pallas_call(partial(fetch_kernel, places), name=name, out_shape=tuple(...  34.1 us
    pallas_call x7, Pallas kernels, weight_gradients(): pl.pallas_call(kernel, grid=(model // 512,), out_shape=pltpu.HBM((model,...  23.5 us
  transfers between devices with their start and end apart: 151, of which 59 were waited for; matrix products, arithmetic and copies ran while one was open for 1% of the time, Pallas kernels for 30%

profile of v1, /device:TPU:1, one launch (start us, length us, event | category | flops | bytes accessed | tf_op | source)
XLA Modules:
  0.0 596.3 jit_solution(7703563485594963541)
XLA Ops:
  24.4 53.9 %all-gather.4.cloned.1.call-done.weight.refs_0_ = bf16[2048,1664]{1,0:T(8,128)(2,1)} async-done(((bf16[128,1664]{1,0:T(8,128)(2,1)}), bf16[2048,1664]{1,0:T(8,128)(2,1)}) %all-gather.4.cloned.1.call-update) | async-done | bytes 6815760 | tf_op jit(solution)/shard_map/all_gather | solution.py:1145
  79.5 5.5 shard_map.289
  103.7 3.9 collective-permute-start.8
  107.7 4.3 collective-permute-start.9
  116.2 6.2 %collective-permute-done.9.msg2.h2 = bf16[528,256]{1,0:T(8,128)(2,1)S(1)} collective-permute-done((bf16[528,256]{1,0:T(8,128)(2,1)S(1)}, bf16[528,256]{1,0:T(8,128)(2,1)S(1)}, u32[]{:S(2)}, u32[]{:S(2)}) %collective-permute-start.9) | collective-permute-done | bytes 270368 | tf_op jit(solution)/shard_map/ppermute | solution.py:45
  122.4 5.7 collective-permute-done.10.msg3.h3
  140.6 5.5 collective-permute-done.13.part1
  160.2 6.7 %all-gather.6.cloned.1.call-done.refs_0_.refs_1_ = bf16[2048,2688]{1,0:T(8,128)(2,1)} async-done(((bf16[128,2688]{1,0:T(8,128)(2,1)}), bf16[2048,2688]{1,0:T(8,128)(2,1)}) %all-gather.6.cloned.1.call-update) | async-done | bytes 11010064 | tf_op jit(solution)/shard_map/all_gather | solution.py:1145
  180.9 3.3 collective-permute-done.24.part1
  185.6 3.5 collective-permute-start.27
  200.0 3.3 shard_map.305
  218.7 4.1 collective-permute-start.42
  222.8 7.1 %collective-permute-start.43 = (bf16[528,256]{1,0:T(8,128)(2,1)S(1)}, bf16[528,256]{1,0:T(8,128)(2,1)S(1)}, u32[]{:S(2)}, u32[]{:S(2)}) collective-permute-start(bf16[528,256]{1,0:T(8,128)(2,1)S(1)} %get-tuple-element.576), channel_id=1, source_target_pairs={{0,16},{8,24},{1,17},{9,25},{2,18},{10,26},{3,19},{11,27},{4,20},{... | collective-permute-start | bytes 811016 | tf_op jit(solution)/shard_map/ppermute | solution.py:45
  234.6 11.6 %collective-permute-done.43.msg2.h2 = bf16[528,256]{1,0:T(8,128)(2,1)S(1)} collective-permute-done((bf16[528,256]{1,0:T(8,128)(2,1)S(1)}, bf16[528,256]{1,0:T(8,128)(2,1)S(1)}, u32[]{:S(2)}, u32[]{:S(2)}) %collective-permute-start.43) | collective-permute-done | bytes 270368 | tf_op jit(solution)/shard_map/ppermute | solution.py:45
  290.9 4.4 shard_map.321.refs_4_
  298.3 3.2 collective-permute-start.61
  322.1 3.7 shard_map.328
  330.5 3.1 shard_map.326.refs_2_
  348.5 4.8 shard_map.330
  383.8 3.2 ffn_again.1
  404.0 4.5 shard_map.341.refs_4_
  411.0 3.5 collective-permute-start.96
  435.5 3.6 shard_map.348
  443.8 3.1 shard_map.346.refs_2_
  450.7 3.7 collective-permute-done.109.kv3
  462.5 4.4 shard_map.350
  489.9 4.9 shard_map.356.block
  499.8 7.2 %all-to-all-start = ((bf16[16,128,768]{2,1,0:T(8,128)(2,1)}), bf16[16,128,768]{2,1,0:T(8,128)(2,1)S(1)}, u32[]{:S(2)}, u32[]{:S(2)}) async-start(bf16[16,128,768]{2,1,0:T(8,128)(2,1)} %shard_map.361), calls=%async_computation.1 | async-start | bytes 6291456 | tf_op jit(solution)/shard_map/all_to_all | solution.py:1399
  514.0 3.7 collective-permute-start.122
  532.1 3.7 collective-permute-start.128
  542.8 19.1 %all-to-all-done.values = bf16[16,128,768]{2,1,0:T(8,128)(2,1)S(1)} async-done(((bf16[16,128,768]{2,1,0:T(8,128)(2,1)}), bf16[16,128,768]{2,1,0:T(8,128)(2,1)S(1)}, u32[]{:S(2)}, u32[]{:S(2)}) %all-to-all-start) | async-done | bytes 3145760 | tf_op jit(solution)/shard_map/all_to_all | solution.py:1399
  578.4 7.4 %reduce-scatter.5.cloned.1.call-done.lower = bf16[128,3072]{1,0:T(8,128)(2,1)} async-done(((bf16[2048,3072]{1,0:T(8,128)(2,1)}), bf16[128,3072]{1,0:T(8,128)(2,1)}) %reduce-scatter.5.cloned.1.call-update) | async-done | bytes 786448 | tf_op jit(solution)/shard_map/reduce_scatter | solution.py:1339
  (501 shorter events, 365.0 us)
Async XLA Ops:
  7.2 71.1 %all-gather.4.cloned.1.call-start = ((), (), s32[]{:S(2)}) async-start(), calls=%async_computation.3 | async-start | bytes 7241728 | tf_op jit(solution)/shard_map/all_gather | solution.py:1145
  11.1 155.8 %all-gather.6.cloned.1.call-start = ((), (), s32[]{:S(2)}) async-start(), calls=%async_computation.4 | async-start | bytes 11698176 | tf_op jit(solution)/shard_map/all_gather | solution.py:1145
  13.7 233.5 %all-gather.8.cloned.1.call-start = ((), (), s32[]{:S(2)}) async-start(), calls=%async_computation.5 | async-start | bytes 8912896 | tf_op jit(solution)/shard_map/all_gather | solution.py:1145
  15.8 438.6 %reduce-scatter.3.cloned.1.call-start = ((), (), s32[]{:S(2)}) async-start(), calls=%async_computation.6 | async-start | bytes 11141120 | tf_op jit(solution)/shard_map/reduce_scatter | solution.py:1342
  103.7 12.4 %collective-permute-start.8 = (bf16[528,256]{1,0:T(8,128)(2,1)S(1)}, bf16[528,256]{1,0:T(8,128)(2,1)S(1)}, u32[]{:S(2)}, u32[]{:S(2)}) collective-permute-start(bf16[528,256]{1,0:T(8,128)(2,1)S(1)} %get-tuple-element.500), channel_id=1, source_target_pairs={{0,8},{8,16},{16,24},{1,9},{9,17},{17,25},{2,10},{10,18},{18,26},{... | collective-permute-start | bytes 811016 | tf_op jit(solution)/shard_map/ppermute | solution.py:45
  107.7 14.7 %collective-permute-start.9 = (bf16[528,256]{1,0:T(8,128)(2,1)S(1)}, bf16[528,256]{1,0:T(8,128)(2,1)S(1)}, u32[]{:S(2)}, u32[]{:S(2)}) collective-permute-start(bf16[528,256]{1,0:T(8,128)(2,1)S(1)} %get-tuple-element.500), channel_id=1, source_target_pairs={{0,16},{8,24},{1,17},{9,25},{2,18},{10,26},{3,19},{11,27},{4,20},{... | collective-permute-start | bytes 811016 | tf_op jit(solution)/shard_map/ppermute | solution.py:45
  112.0 16.1 %collective-permute-start.10 = (bf16[528,256]{1,0:T(8,128)(2,1)S(1)}, bf16[528,256]{1,0:T(8,128)(2,1)S(1)}, u32[]{:S(2)}, u32[]{:S(2)}) collective-permute-start(bf16[528,256]{1,0:T(8,128)(2,1)S(1)} %get-tuple-element.500), channel_id=1, source_target_pairs={{0,24},{1,25},{2,26},{3,27},{4,28},{5,29},{6,30},{7,31},{32,56},{3... | collective-permute-start | bytes 811016 | tf_op jit(solution)/shard_map/ppermute | solution.py:45
  150.9 18.9 %collective-permute-start.19 = (bf16[32,2048]{1,0:T(8,128)(2,1)S(1)}, bf16[32,2048]{1,0:T(8,128)(2,1)S(1)}, u32[]{:S(2)}, u32[]{:S(2)}) collective-permute-start(bf16[32,2048]{1,0:T(8,128)(2,1)S(1)} %get-tuple-element.524.p0), channel_id=1, source_target_pairs={{0,1},{1,0},{2,3},{3,2},{4,5},{5,4},{6,7},{7,6},{8,9},{9,8},{10,11... | collective-permute-start | bytes 393224 | tf_op jit(solution)/shard_map/ppermute | solution.py:40
  153.9 15.9 %collective-permute-start.20 = (bf16[32,2048]{1,0:T(8,128)(2,1)S(1)}, bf16[32,2048]{1,0:T(8,128)(2,1)S(1)}, u32[]{:S(2)}, u32[]{:S(2)}) collective-permute-start(bf16[32,2048]{1,0:T(8,128)(2,1)S(1)} %collective-permute-done.16.p1), channel_id=1, source_target_pairs={{0,1},{1,0},{2,3},{3,2},{4,5},{5,4},{6,7},{7,6},{8,9},{9,8},{10,11... | collective-permute-start | bytes 393224 | tf_op jit(solution)/shard_map/ppermute | solution.py:40
  156.8 13.0 %collective-permute-start.21 = (bf16[32,2048]{1,0:T(8,128)(2,1)S(1)}, bf16[32,2048]{1,0:T(8,128)(2,1)S(1)}, u32[]{:S(2)}, u32[]{:S(2)}) collective-permute-start(bf16[32,2048]{1,0:T(8,128)(2,1)S(1)} %collective-permute-done.17.p2), channel_id=1, source_target_pairs={{0,1},{1,0},{2,3},{3,2},{4,5},{5,4},{6,7},{7,6},{8,9},{9,8},{10,11... | collective-permute-start | bytes 393224 | tf_op jit(solution)/shard_map/ppermute | solution.py:40
  159.4 10.4 %collective-permute-start.22 = (bf16[32,2048]{1,0:T(8,128)(2,1)S(1)}, bf16[32,2048]{1,0:T(8,128)(2,1)S(1)}, u32[]{:S(2)}, u32[]{:S(2)}) collective-permute-start(bf16[32,2048]{1,0:T(8,128)(2,1)S(1)} %collective-permute-done.18.p3), channel_id=1, source_target_pairs={{0,1},{1,0},{2,3},{3,2},{4,5},{5,4},{6,7},{7,6},{8,9},{9,8},{10,11... | collective-permute-start | bytes 393224 | tf_op jit(solution)/shard_map/ppermute | solution.py:40
  218.7 15.9 %collective-permute-start.42 = (bf16[528,256]{1,0:T(8,128)(2,1)S(1)}, bf16[528,256]{1,0:T(8,128)(2,1)S(1)}, u32[]{:S(2)}, u32[]{:S(2)}) collective-permute-start(bf16[528,256]{1,0:T(8,128)(2,1)S(1)} %get-tuple-element.576), channel_id=1, source_target_pairs={{0,8},{8,16},{16,24},{1,9},{9,17},{17,25},{2,10},{10,18},{18,26},{... | collective-permute-start | bytes 811016 | tf_op jit(solution)/shard_map/ppermute | solution.py:45
  222.8 23.3 %collective-permute-start.43 = (bf16[528,256]{1,0:T(8,128)(2,1)S(1)}, bf16[528,256]{1,0:T(8,128)(2,1)S(1)}, u32[]{:S(2)}, u32[]{:S(2)}) collective-permute-start(bf16[528,256]{1,0:T(8,128)(2,1)S(1)} %get-tuple-element.576), channel_id=1, source_target_pairs={{0,16},{8,24},{1,17},{9,25},{2,18},{10,26},{3,19},{11,27},{4,20},{... | collective-permute-start | bytes 811016 | tf_op jit(solution)/shard_map/ppermute | solution.py:45
  229.9 16.2 %collective-permute-start.44 = (bf16[528,256]{1,0:T(8,128)(2,1)S(1)}, bf16[528,256]{1,0:T(8,128)(2,1)S(1)}, u32[]{:S(2)}, u32[]{:S(2)}) collective-permute-start(bf16[528,256]{1,0:T(8,128)(2,1)S(1)} %get-tuple-element.576), channel_id=1, source_target_pairs={{0,24},{1,25},{2,26},{3,27},{4,28},{5,29},{6,30},{7,31},{32,56},{3... | collective-permute-start | bytes 811016 | tf_op jit(solution)/shard_map/ppermute | solution.py:45
  315.0 14.1 %collective-permute-start.68 = (bf16[400,256]{1,0:T(8,128)(2,1)S(1)}, bf16[400,256]{1,0:T(8,128)(2,1)S(1)}, u32[]{:S(2)}, u32[]{:S(2)}) collective-permute-start(bf16[400,256]{1,0:T(8,128)(2,1)S(1)} %get-tuple-element.677), channel_id=1, source_target_pairs={{8,0},{16,8},{24,16},{9,1},{17,9},{25,17},{10,2},{18,10},{26,18},{... | collective-permute-start | bytes 614408 | tf_op jit(solution)/shard_map/ppermute | solution.py:45
  316.3 20.1 %collective-permute-start.69 = (bf16[400,256]{1,0:T(8,128)(2,1)S(1)}, bf16[400,256]{1,0:T(8,128)(2,1)}, u32[]{:S(2)}, u32[]{:S(2)}) collective-permute-start(bf16[400,256]{1,0:T(8,128)(2,1)S(1)} %get-tuple-element.677), channel_id=1, source_target_pairs={{16,0},{24,8},{17,1},{25,9},{18,2},{26,10},{19,3},{27,11},{20,4},{... | collective-permute-start | bytes 614408 | tf_op jit(solution)/shard_map/ppermute | solution.py:45
  317.6 18.8 %collective-permute-start.70 = (bf16[400,256]{1,0:T(8,128)(2,1)S(1)}, bf16[400,256]{1,0:T(8,128)(2,1)}, u32[]{:S(2)}, u32[]{:S(2)}) collective-permute-start(bf16[400,256]{1,0:T(8,128)(2,1)S(1)} %get-tuple-element.677), channel_id=1, source_target_pairs={{24,0},{25,1},{26,2},{27,3},{28,4},{29,5},{30,6},{31,7},{56,32},{5... | collective-permute-start | bytes 614408 | tf_op jit(solution)/shard_map/ppermute | solution.py:45
  326.5 9.9 %collective-permute-start.72 = (bf16[256,128]{1,0:T(8,128)(2,1)S(1)}, bf16[256,128]{1,0:T(8,128)(2,1)S(1)}, u32[]{:S(2)}, u32[]{:S(2)}) collective-permute-start(bf16[256,128]{1,0:T(8,128)(2,1)S(1)} %get-tuple-element.681), channel_id=1, source_target_pairs={{8,0},{16,8},{24,16},{9,1},{17,9},{25,17},{10,2},{18,10},{26,18},{... | collective-permute-start | bytes 196616 | tf_op jit(solution)/shard_map/ppermute | solution.py:45
  329.1 10.8 %collective-permute-start.74 = (bf16[256,128]{1,0:T(8,128)(2,1)S(1)}, bf16[256,128]{1,0:T(8,128)(2,1)S(1)}, u32[]{:S(2)}, u32[]{:S(2)}) collective-permute-start(bf16[256,128]{1,0:T(8,128)(2,1)S(1)} %get-tuple-element.683), channel_id=1, source_target_pairs={{24,0},{25,1},{26,2},{27,3},{28,4},{29,5},{30,6},{31,7},{56,32},{5... | collective-permute-start | bytes 196616 | tf_op jit(solution)/shard_map/ppermute | solution.py:45
  340.5 245.2 %reduce-scatter.5.cloned.1.call-start = ((), (), s32[]{:S(2)}) async-start(), calls=%async_computation.7 | async-start | bytes 13369344 | tf_op jit(solution)/shard_map/reduce_scatter | solution.py:1339
  379.7 9.7 %collective-permute-start.85 = (bf16[32,2048]{1,0:T(8,128)(2,1)S(1)}, bf16[32,2048]{1,0:T(8,128)(2,1)S(1)}, u32[]{:S(2)}, u32[]{:S(2)}) collective-permute-start(bf16[32,2048]{1,0:T(8,128)(2,1)S(1)} %get-tuple-element.746.refs_0_), channel_id=1, source_target_pairs={{0,6},{1,7},{2,0},{3,1},{4,2},{5,3},{6,4},{7,5},{8,14},{9,15},{10,... | collective-permute-start | bytes 393224 | tf_op jit(solution)/shard_map/ppermute | solution.py:36
  428.0 14.5 %collective-permute-start.103 = (bf16[400,256]{1,0:T(8,128)(2,1)S(1)}, bf16[400,256]{1,0:T(8,128)(2,1)S(1)}, u32[]{:S(2)}, u32[]{:S(2)}) collective-permute-start(bf16[400,256]{1,0:T(8,128)(2,1)S(1)} %get-tuple-element.822), channel_id=1, source_target_pairs={{8,0},{16,8},{24,16},{9,1},{17,9},{25,17},{10,2},{18,10},{26,18},{... | collective-permute-start | bytes 614408 | tf_op jit(solution)/shard_map/ppermute | solution.py:45
  429.3 20.4 %collective-permute-start.104 = (bf16[400,256]{1,0:T(8,128)(2,1)S(1)}, bf16[400,256]{1,0:T(8,128)(2,1)}, u32[]{:S(2)}, u32[]{:S(2)}) collective-permute-start(bf16[400,256]{1,0:T(8,128)(2,1)S(1)} %get-tuple-element.822), channel_id=1, source_target_pairs={{16,0},{24,8},{17,1},{25,9},{18,2},{26,10},{19,3},{27,11},{20,4},{... | collective-permute-start | bytes 614408 | tf_op jit(solution)/shard_map/ppermute | solution.py:45
  430.6 19.1 %collective-permute-start.105 = (bf16[400,256]{1,0:T(8,128)(2,1)S(1)}, bf16[400,256]{1,0:T(8,128)(2,1)}, u32[]{:S(2)}, u32[]{:S(2)}) collective-permute-start(bf16[400,256]{1,0:T(8,128)(2,1)S(1)} %get-tuple-element.822), channel_id=1, source_target_pairs={{24,0},{25,1},{26,2},{27,3},{28,4},{29,5},{30,6},{31,7},{56,32},{5... | collective-permute-start | bytes 614408 | tf_op jit(solution)/shard_map/ppermute | solution.py:45
  439.9 9.9 %collective-permute-start.107 = (bf16[256,128]{1,0:T(8,128)(2,1)}, bf16[256,128]{1,0:T(8,128)(2,1)}, u32[]{:S(2)}, u32[]{:S(2)}) collective-permute-start(bf16[256,128]{1,0:T(8,128)(2,1)} %get-tuple-element.826), channel_id=1, source_target_pairs={{8,0},{16,8},{24,16},{9,1},{17,9},{25,17},{10,2},{18,10},{26,18},{... | collective-permute-start | bytes 196616 | tf_op jit(solution)/shard_map/ppermute | solution.py:45
  442.5 12.0 %collective-permute-start.109 = (bf16[256,128]{1,0:T(8,128)(2,1)S(1)}, bf16[256,128]{1,0:T(8,128)(2,1)}, u32[]{:S(2)}, u32[]{:S(2)}) collective-permute-start(bf16[256,128]{1,0:T(8,128)(2,1)S(1)} %get-tuple-element.828), channel_id=1, source_target_pairs={{24,0},{25,1},{26,2},{27,3},{28,4},{29,5},{30,6},{31,7},{56,32},{5... | collective-permute-start | bytes 196616 | tf_op jit(solution)/shard_map/ppermute | solution.py:45
  483.4 11.4 %collective-permute-start.117 = (bf16[32,2048]{1,0:T(8,128)(2,1)S(1)}, bf16[32,2048]{1,0:T(8,128)(2,1)S(1)}, u32[]{:S(2)}, u32[]{:S(2)}) collective-permute-start(bf16[32,2048]{1,0:T(8,128)(2,1)S(1)} %get-tuple-element.872), channel_id=1, source_target_pairs={{0,2},{1,3},{2,4},{3,5},{4,6},{5,7},{6,0},{7,1},{8,10},{9,11},{10,... | collective-permute-start | bytes 393224 | tf_op jit(solution)/shard_map/ppermute | solution.py:36
  484.1 10.7 %collective-permute-start.118 = (bf16[32,2048]{1,0:T(8,128)(2,1)S(1)}, bf16[32,2048]{1,0:T(8,128)(2,1)S(1)}, u32[]{:S(2)}, u32[]{:S(2)}) collective-permute-start(bf16[32,2048]{1,0:T(8,128)(2,1)S(1)} %get-tuple-element.873), channel_id=1, source_target_pairs={{0,4},{1,5},{2,6},{3,7},{4,0},{5,1},{6,2},{7,3},{8,12},{9,13},{10,... | collective-permute-start | bytes 393224 | tf_op jit(solution)/shard_map/ppermute | solution.py:36
  499.8 62.2 %all-to-all-start = ((bf16[16,128,768]{2,1,0:T(8,128)(2,1)}), bf16[16,128,768]{2,1,0:T(8,128)(2,1)S(1)}, u32[]{:S(2)}, u32[]{:S(2)}) async-start(bf16[16,128,768]{2,1,0:T(8,128)(2,1)} %shard_map.361), calls=%async_computation.1 | async-start | bytes 6291456 | tf_op jit(solution)/shard_map/all_to_all | solution.py:1399
  517.8 11.4 %collective-permute-start.133 = (bf16[32,2048]{1,0:T(8,128)(2,1)S(1)}, bf16[32,2048]{1,0:T(8,128)(2,1)S(1)}, u32[]{:S(2)}, u32[]{:S(2)}) collective-permute-start(bf16[32,2048]{1,0:T(8,128)(2,1)S(1)} %get-tuple-element.913.p0), channel_id=1, source_target_pairs={{0,2},{1,3},{2,4},{3,5},{4,6},{5,7},{6,0},{7,1},{8,10},{9,11},{10,... | collective-permute-start | bytes 393224 | tf_op jit(solution)/shard_map/ppermute | solution.py:36
  519.1 10.1 %collective-permute-start.134 = (bf16[32,2048]{1,0:T(8,128)(2,1)S(1)}, bf16[32,2048]{1,0:T(8,128)(2,1)S(1)}, u32[]{:S(2)}, u32[]{:S(2)}) collective-permute-start(bf16[32,2048]{1,0:T(8,128)(2,1)S(1)} %get-tuple-element.913.p0), channel_id=1, source_target_pairs={{0,1},{1,0},{2,3},{3,2},{4,5},{5,4},{6,7},{7,6},{8,9},{9,8},{10,11... | collective-permute-start | bytes 393224 | tf_op jit(solution)/shard_map/ppermute | solution.py:40
  530.9 10.4 %collective-permute-start.127 = (bf16[32,2048]{1,0:T(8,128)(2,1)S(1)}, bf16[32,2048]{1,0:T(8,128)(2,1)S(1)}, u32[]{:S(2)}, u32[]{:S(2)}) collective-permute-start(bf16[32,2048]{1,0:T(8,128)(2,1)S(1)} %shard_map.364.p0), channel_id=1, source_target_pairs={{0,1},{1,0},{2,3},{3,2},{4,5},{5,4},{6,7},{7,6},{8,9},{9,8},{10,11... | collective-permute-start | bytes 393224 | tf_op jit(solution)/shard_map/ppermute | solution.py:40
  (153 other events, 1622.8 us)
Sparse Core Ops, SparseCore 0:
  11.2 67.0 all-gather.3
  81.0 85.8 all-gather.5
  169.0 76.9 all-gather.7
  340.1 89.3 reduce-scatter.2
  454.6 131.1 reduce-scatter.4
